TPU v7x, 256 devices: a whole 4x4x8 slice. The times are simulated.
256 devices in a mesh: sub: 8 (over z_hi, x), strip: 32 (over y, z_lo, core).
Axes of the slice: x: 4, y: 4, z: 8 (z_hi: 2, z_lo: 4; z = z_hi * 4 + z_lo), core: 2. Of those that a mesh axis runs over, the one named last changes fastest.
Arguments:
- forcing: float32 [8, 2048, 2048], P('sub', 'strip'), may hold values from -6 to 6
- mult_start: float32 [8, 2048, 2048], P('sub', 'strip'), may hold values from -6 to 6
- incr_start: float32 [8, 2048, 2048], P('sub', 'strip'), may hold values from -6 to 6
- diffusivity: float32 [8, 2048, 2048], P('sub', 'strip'), may hold values from 0.02 to 0.24
- north_corr: bfloat16 [2048, 2048], P('strip'), may hold values from -0.07629126 to 1.07629126
- east_corr: bfloat16 [2048, 2048], replicated, may hold values from -0.07629126 to 1.07629126
Outputs:
- mult_resid: float32 [8, 2048, 2048], P('sub', 'strip')
- grad_resid: float32 [8, 2048, 2048], P('sub', 'strip')
All inputs are finite; a program needn't handle non-finite values.
Results may differ from a plain program's by a relative error of at most 0.014.
Values may be sent and summed in bfloat16 or wider, within the bound.
A program may use at most 128 MiB of HBM per device.

v0:
```python
import jax
import jax.numpy as jnp
from jax import lax
from jax.sharding import PartitionSpec as P

STEPS = 4
ITERS = 2


step_weight = 0.5


def shortened(value):
    return jax.tree.map(lambda a: a.astype(jnp.bfloat16) if a.dtype == jnp.float32 else a, value)


def with_halo(value, sides, width):
    for axis, dim in sides:
        size, length = (lax.axis_size(axis), value.shape[dim])
        up = [(i, (i + 1) % size) for i in range(size - 1)]
        down = [(j, i) for i, j in up]
        last = lax.slice_in_dim(value, length - width, length, axis=dim)
        leading = lax.slice_in_dim(value, 0, width, axis=dim)
        before = lax.ppermute(last, axis, up)
        after = lax.ppermute(leading, axis, down)
        value = jnp.concatenate([before, value, after], axis=dim)
    return value


def shifted(value, axis, steps):
    count = lax.axis_size(axis)
    leading, last = (max(0, -steps), min(count, count - steps))
    return lax.ppermute(value, axis, [(source, source + steps) for source in range(leading, last)])


def laplace(padded):
    widened = jnp.pad(padded, ((0, 0), (1, 1)))
    return (
        widened[:-2, 1:-1]
        + widened[2:, 1:-1]
        + widened[1:-1, :-2]
        + widened[1:-1, 2:]
        - 4.0 * widened[1:-1, 1:-1]
    )


def rim_whole(field):
    return with_halo(shortened(field), (("strip", 0),), STEPS).astype(field.dtype)


def local(forcing, mult_start, incr_start, diffusivity, north_corr, east_corr):
    forcing = forcing[0]
    diffuse = diffusivity[0]
    row_count = forcing.shape[0]
    diffuse_wide = with_halo(diffuse.astype(jnp.bfloat16), (("strip", 0),), STEPS).astype(
        diffuse.dtype
    )
    global_rows = (
        lax.axis_index("strip") * row_count - STEPS + lax.iota(jnp.int32, row_count + 2 * STEPS)
    )
    inside = ((global_rows >= 0) & (global_rows < row_count * lax.axis_size("strip"))).astype(
        jnp.float32
    )[:, None]

    def propagate(field):
        widened = rim_whole(field)
        for each_step in range(STEPS):
            length = widened.shape[0] - 2
            spread = laplace(widened)
            coef_part = diffuse_wide[each_step + 1 : each_step + 1 + length]
            widened = (widened[1:-1] + coef_part * spread) * inside[
                each_step + 1 : each_step + 1 + length
            ]
        return widened

    def adjoint(field):
        widened = rim_whole(field)
        for each_step in range(STEPS):
            length = widened.shape[0] - 2
            weighted = diffuse_wide[each_step : each_step + widened.shape[0]] * widened
            widened = (widened[1:-1] + laplace(weighted)) * inside[
                each_step + 1 : each_step + 1 + length
            ]
        return widened

    def forward_op(increment):
        arrived = shifted(shortened(propagate(increment)), "sub", 1)
        return increment - arrived

    def backward_op(multiplier):
        following = shifted(shortened(multiplier), "sub", -1).astype(multiplier.dtype)
        return multiplier - adjoint(following)

    def add_rows(shard_rows):
        return jnp.dot(north_corr, shard_rows, preferred_element_type=jnp.float32)

    def correlate(field):
        lowered = field.astype(jnp.bfloat16)
        north_half = add_rows(lax.all_gather(lowered, "strip", axis=0, tiled=True))
        return jnp.dot(
            north_half.astype(jnp.bfloat16), east_corr, preferred_element_type=jnp.float32
        )

    multiplier = mult_start[0]
    increment = incr_start[0]
    for iteration in range(ITERS):
        multiplier = multiplier + step_weight * (
            forcing - correlate(multiplier) - forward_op(increment)
        )
        increment = increment + step_weight * backward_op(multiplier)
    mult_resid = forcing - correlate(multiplier) - forward_op(increment)
    grad_resid = backward_op(multiplier)
    return (mult_resid[None], grad_resid[None])


def solution(mesh):
    return jax.shard_map(
        local,
        mesh=mesh,
        in_specs=(
            P("sub", "strip", None),
            P("sub", "strip", None),
            P("sub", "strip", None),
            P("sub", "strip", None),
            P("strip", None),
            P(),
        ),
        out_specs=(P("sub", "strip", None), P("sub", "strip", None)),
        check_vma=False,
    )
```

profile of v0, /device:TPU:7, one launch (start us, length us, event | category | flops | bytes accessed | tf_op | source)
XLA Modules:
  0.0 282.3 jit_solution(6523081633490426358)
XLA Ops:
  7.2 1.8 bitcast_convert_fusion.1
  9.1 1.1 convert_element_type.116
  10.2 4.1 %collective-permute-start.2 = (bf16[4,2048]{1,0:T(4,128)(2,1)S(1)}, bf16[4,2048]{1,0:T(4,128)(2,1)S(1)}, u32[]{:S(2)}, u32[]{:S(2)}) collective-permute-start(bf16[4,2048]{1,0:T(4,128)(2,1)S(1)} %get-tuple-element.26), channel_id=1, source_target_pairs={{0,1},{1,2},{2,3},{3,4},{4,5},{5,6},{6,7},{7,8},{8,9},{9,10},{10,1... | collective-permute-start | bytes 49160 | tf_op jit(solution)/shard_map/ppermute | solution.py:24
  14.4 2.1 collective-permute-start.3
  16.4 1.1 bitcast_convert_fusion
  17.5 3.6 %collective-permute-start = (bf16[4,2048]{1,0:T(4,128)(2,1)S(1)}, bf16[4,2048]{1,0:T(4,128)(2,1)S(1)}, u32[]{:S(2)}, u32[]{:S(2)}) collective-permute-start(bf16[4,2048]{1,0:T(4,128)(2,1)S(1)} %get-tuple-element.28), channel_id=1, source_target_pairs={{0,1},{1,2},{2,3},{3,4},{4,5},{5,6},{6,7},{7,8},{8,9},{9,10},{10,1... | collective-permute-start | bytes 49160 | tf_op jit(solution)/shard_map/ppermute | solution.py:24
  21.2 1.9 collective-permute-start.1
  23.1 1.1 convert_bitcast_fusion
  24.5 1.7 collective-permute-done.1
  27.4 0.5 fusion.17
  28.4 8.4 %collective-permute-start.4 = (bf16[64,2048]{1,0:T(8,128)(2,1)S(1)}, bf16[64,2048]{1,0:T(8,128)(2,1)S(1)}, u32[]{:S(2)}, u32[]{:S(2)}) collective-permute-start(bf16[64,2048]{1,0:T(8,128)(2,1)S(1)} %fusion.90), channel_id=1, source_target_pairs={{0,32},{32,64},{64,96},{96,128},{128,160},{160,192},{192,224},{1,3... | collective-permute-start | bytes 786440 | tf_op jit(solution)/shard_map/ppermute | solution.py:33
  36.8 10.3 %collective-permute-done.4 = bf16[64,2048]{1,0:T(8,128)(2,1)S(1)} collective-permute-done((bf16[64,2048]{1,0:T(8,128)(2,1)S(1)}, bf16[64,2048]{1,0:T(8,128)(2,1)S(1)}, u32[]{:S(2)}, u32[]{:S(2)}) %collective-permute-start.4) | collective-permute-done | bytes 262176 | tf_op jit(solution)/shard_map/ppermute | solution.py:33
  47.0 44.8 %all-gather.4.cloned.1.call-done = bf16[2048,2048]{1,0:T(8,128)(2,1)} async-done(((bf16[64,2048]{1,0:T(8,128)(2,1)}), bf16[2048,2048]{1,0:T(8,128)(2,1)}) %all-gather.4.cloned.1.call-update) | async-done | bytes 8388624 | tf_op jit(solution)/shard_map/all_gather | solution.py:99
  91.8 9.6 %fusion.125 = (bf16[64,2048]{1,0:T(8,128)(2,1)}, f32[64,2048]{1,0:T(8,128)S(1)}) fusion(bf16[64,2048]{1,0:T(8,128)(2,1)S(1)} %collective-permute-done.4, f32[1,64,2048]{2,1,0:T(8,128)S(1)} %copy-done.2, f32[1,64,2048]{2,1,0:T(8,128)S(1)} %copy-done.1, bf16[2048,2048]{1,0:T(8,128)(2,1)} %param.11, bf16[64,2048]{1,0:T(8,128)(2,1)S(1)} %copy-done, ...), kind=kOutput, calls=%fused_computation.204 | convolution fusion | flops 1074790400 | bytes 19660800 | tf_op jit(solution)/shard_map/dot_general | solution.py:100
  101.4 2.1 collective-permute-start.5
  103.5 15.5 %collective-permute-done.5 = bf16[64,2048]{1,0:T(8,128)(2,1)S(1)} collective-permute-done((bf16[64,2048]{1,0:T(8,128)(2,1)}, bf16[64,2048]{1,0:T(8,128)(2,1)S(1)}, u32[]{:S(2)}, u32[]{:S(2)}) %collective-permute-start.5) | collective-permute-done | bytes 262176 | tf_op jit(solution)/shard_map/ppermute | solution.py:33
  119.0 13.1 %collective-permute-start.6 = (bf16[4,2048]{1,0:T(4,128)(2,1)S(1)}, bf16[4,2048]{1,0:T(4,128)(2,1)S(1)}, u32[]{:S(2)}, u32[]{:S(2)}) collective-permute-start(bf16[4,2048]{1,0:T(4,128)(2,1)S(1)} %get-tuple-element.24), channel_id=1, source_target_pairs={{0,1},{1,2},{2,3},{3,4},{4,5},{5,6},{6,7},{7,8},{8,9},{9,10},{10,1... | collective-permute-start | bytes 49160 | tf_op jit(solution)/shard_map/ppermute | solution.py:24
  132.1 1.9 collective-permute-start.7
  134.0 3.5 %collective-permute-done.7 = bf16[4,2048]{1,0:T(4,128)(2,1)S(1)} collective-permute-done((bf16[4,2048]{1,0:T(4,128)(2,1)S(1)}, bf16[4,2048]{1,0:T(4,128)(2,1)S(1)}, u32[]{:S(2)}, u32[]{:S(2)}) %collective-permute-start.7) | collective-permute-done | bytes 16416 | tf_op jit(solution)/shard_map/ppermute | solution.py:25
  137.8 0.6 slice_multiply_fusion.13
  138.4 0.6 slice_multiply_fusion.11
  138.9 0.6 slice_multiply_fusion.9
  139.5 0.5 fusion.133
  140.1 1.9 collective-permute-start.8
  142.0 2.4 collective-permute-start.9
  144.4 3.2 %collective-permute-done.9 = bf16[4,2048]{1,0:T(4,128)(2,1)S(1)} collective-permute-done((bf16[4,2048]{1,0:T(4,128)(2,1)S(1)}, bf16[4,2048]{1,0:T(4,128)(2,1)S(1)}, u32[]{:S(2)}, u32[]{:S(2)}) %collective-permute-start.9) | collective-permute-done | bytes 16416 | tf_op jit(solution)/shard_map/ppermute | solution.py:25
  148.7 0.5 fusion.50
  149.7 2.1 collective-permute-start.10
  151.8 8.7 %collective-permute-done.10 = bf16[64,2048]{1,0:T(8,128)(2,1)} collective-permute-done((bf16[64,2048]{1,0:T(8,128)(2,1)S(1)}, bf16[64,2048]{1,0:T(8,128)(2,1)}, u32[]{:S(2)}, u32[]{:S(2)}) %collective-permute-start.10) | collective-permute-done | bytes 262176 | tf_op jit(solution)/shard_map/ppermute | solution.py:33
  160.5 15.8 %all-gather.6.cloned.1.call-done = bf16[2048,2048]{1,0:T(8,128)(2,1)} async-done(((bf16[64,2048]{1,0:T(8,128)(2,1)}), bf16[2048,2048]{1,0:T(8,128)(2,1)}) %all-gather.6.cloned.1.call-update) | async-done | bytes 8388624 | tf_op jit(solution)/shard_map/all_gather | solution.py:99
  176.3 12.2 %fusion.143 = (bf16[64,2048]{1,0:T(8,128)(2,1)}, f32[64,2048]{1,0:T(8,128)}) fusion(f32[64,2048]{1,0:T(8,128)S(1)} %get-tuple-element.11, bf16[64,2048]{1,0:T(8,128)(2,1)} %collective-permute-done.10, bf16[2048,2048]{1,0:T(8,128)(2,1)} %param.11, bf16[2048,2048]{1,0:T(8,128)(2,1)} %all-gather.6.cloned.1.call-done, bf16[64,2048]{1,0:T(8,128)(2,1)S(1)} %copy-done, ...), kind=kOutput, calls=%fused_computation.229 | convolution fusion | flops 1075445760 | bytes 20971520 | tf_op jit(solution)/shard_map/dot_general | solution.py:100
  188.6 2.1 collective-permute-start.11
  190.6 15.1 %collective-permute-done.11 = bf16[64,2048]{1,0:T(8,128)(2,1)S(1)} collective-permute-done((bf16[64,2048]{1,0:T(8,128)(2,1)}, bf16[64,2048]{1,0:T(8,128)(2,1)S(1)}, u32[]{:S(2)}, u32[]{:S(2)}) %collective-permute-start.11) | collective-permute-done | bytes 262176 | tf_op jit(solution)/shard_map/ppermute | solution.py:33
  205.7 13.4 %collective-permute-start.12 = (bf16[4,2048]{1,0:T(4,128)(2,1)S(1)}, bf16[4,2048]{1,0:T(4,128)(2,1)S(1)}, u32[]{:S(2)}, u32[]{:S(2)}) collective-permute-start(bf16[4,2048]{1,0:T(4,128)(2,1)S(1)} %get-tuple-element.20), channel_id=1, source_target_pairs={{0,1},{1,2},{2,3},{3,4},{4,5},{5,6},{6,7},{7,8},{8,9},{9,10},{10,1... | collective-permute-start | bytes 49160 | tf_op jit(solution)/shard_map/ppermute | solution.py:24
  219.2 1.9 collective-permute-start.13
  221.1 3.7 %collective-permute-done.13 = bf16[4,2048]{1,0:T(4,128)(2,1)S(1)} collective-permute-done((bf16[4,2048]{1,0:T(4,128)(2,1)S(1)}, bf16[4,2048]{1,0:T(4,128)(2,1)S(1)}, u32[]{:S(2)}, u32[]{:S(2)}) %collective-permute-start.13) | collective-permute-done | bytes 16416 | tf_op jit(solution)/shard_map/ppermute | solution.py:25
  224.9 1.1 fusion.127
  226.0 0.6 slice_multiply_fusion.12
  226.6 0.6 slice_multiply_fusion.10
  227.1 0.6 slice_multiply_fusion.8
  227.7 1.3 fusion.126
  229.0 1.9 collective-permute-start.14
  230.9 2.4 collective-permute-start.15
  233.3 3.1 %collective-permute-done.15 = bf16[4,2048]{1,0:T(4,128)(2,1)S(1)} collective-permute-done((bf16[4,2048]{1,0:T(4,128)(2,1)S(1)}, bf16[4,2048]{1,0:T(4,128)(2,1)S(1)}, u32[]{:S(2)}, u32[]{:S(2)}) %collective-permute-start.15) | collective-permute-done | bytes 16416 | tf_op jit(solution)/shard_map/ppermute | solution.py:25
  238.5 2.3 collective-permute-start.16
  240.8 22.7 %all-gather.8.cloned.1.call-done = bf16[2048,2048]{1,0:T(8,128)(2,1)} async-done(((bf16[64,2048]{1,0:T(8,128)(2,1)}), bf16[2048,2048]{1,0:T(8,128)(2,1)}) %all-gather.8.cloned.1.call-update) | async-done | bytes 8388624 | tf_op jit(solution)/shard_map/all_gather | solution.py:99
  263.5 11.3 %convolution_subtract_fusion = f32[64,2048]{1,0:T(8,128)S(1)} fusion(bf16[2048,2048]{1,0:T(8,128)(2,1)} %param.11, bf16[2048,2048]{1,0:T(8,128)(2,1)} %all-gather.8.cloned.1.call-done, bf16[64,2048]{1,0:T(8,128)(2,1)S(1)} %copy-done, f32[1,64,2048]{2,1,0:T(8,128)S(1)} %copy-done.3), kind=kOutput, calls=%fused_computation.2 | convolution fusion | flops 1074003968 | bytes 18087936 | tf_op jit(solution)/shard_map/dot_general | solution.py:100
  274.9 0.9 subtract_bitcast_fusion
  (60 shorter events, 6.1 us)
Async XLA Ops:
  7.2 84.6 %copy-start = (bf16[64,2048]{1,0:T(8,128)(2,1)S(1)}, bf16[64,2048]{1,0:T(8,128)(2,1)}, u32[]{:S(2)}) copy-start(bf16[64,2048]{1,0:T(8,128)(2,1)} %param.10) | copy-start | bytes 786436
  7.2 84.6 %all-gather.4.cloned.1.call-start = ((), (), s32[]{:S(2)}) async-start(), calls=%async_computation | async-start | bytes 8650752 | tf_op jit(solution)/shard_map/all_gather | solution.py:99
  9.1 167.3 %all-gather.6.cloned.1.call-start = ((), (), s32[]{:S(2)}) async-start(), calls=%async_computation.1 | async-start | bytes 8650752 | tf_op jit(solution)/shard_map/all_gather | solution.py:99
  10.2 16.1 %collective-permute-start.2 = (bf16[4,2048]{1,0:T(4,128)(2,1)S(1)}, bf16[4,2048]{1,0:T(4,128)(2,1)S(1)}, u32[]{:S(2)}, u32[]{:S(2)}) collective-permute-start(bf16[4,2048]{1,0:T(4,128)(2,1)S(1)} %get-tuple-element.26), channel_id=1, source_target_pairs={{0,1},{1,2},{2,3},{3,4},{4,5},{5,6},{6,7},{7,8},{8,9},{9,10},{10,1... | collective-permute-start | bytes 49160 | tf_op jit(solution)/shard_map/ppermute | solution.py:24
  14.3 77.5 %copy-start.1 = (f32[1,64,2048]{2,1,0:T(8,128)S(1)}, f32[1,64,2048]{2,1,0:T(8,128)}, u32[]{:S(2)}) copy-start(f32[1,64,2048]{2,1,0:T(8,128)} %param.7) | copy-start | bytes 1572868
  14.3 77.5 %copy-start.2 = (f32[1,64,2048]{2,1,0:T(8,128)S(1)}, f32[1,64,2048]{2,1,0:T(8,128)}, u32[]{:S(2)}) copy-start(f32[1,64,2048]{2,1,0:T(8,128)} %param.8) | copy-start | bytes 1572868
  14.3 77.4 %copy-start.3 = (f32[1,64,2048]{2,1,0:T(8,128)S(1)}, f32[1,64,2048]{2,1,0:T(8,128)}, u32[]{:S(2)}) copy-start(f32[1,64,2048]{2,1,0:T(8,128)} %param.6) | copy-start | bytes 1572868
  14.4 12.0 %collective-permute-start.3 = (bf16[4,2048]{1,0:T(4,128)(2,1)S(1)}, bf16[4,2048]{1,0:T(4,128)(2,1)S(1)}, u32[]{:S(2)}, u32[]{:S(2)}) collective-permute-start(bf16[4,2048]{1,0:T(4,128)(2,1)S(1)} %get-tuple-element.27), channel_id=1, source_target_pairs={{1,0},{2,1},{3,2},{4,3},{5,4},{6,5},{7,6},{8,7},{9,8},{10,9},{11,1... | collective-permute-start | bytes 49160 | tf_op jit(solution)/shard_map/ppermute | solution.py:25
  17.5 7.0 %collective-permute-start = (bf16[4,2048]{1,0:T(4,128)(2,1)S(1)}, bf16[4,2048]{1,0:T(4,128)(2,1)S(1)}, u32[]{:S(2)}, u32[]{:S(2)}) collective-permute-start(bf16[4,2048]{1,0:T(4,128)(2,1)S(1)} %get-tuple-element.28), channel_id=1, source_target_pairs={{0,1},{1,2},{2,3},{3,4},{4,5},{5,6},{6,7},{7,8},{8,9},{9,10},{10,1... | collective-permute-start | bytes 49160 | tf_op jit(solution)/shard_map/ppermute | solution.py:24
  21.2 5.1 %collective-permute-start.1 = (bf16[4,2048]{1,0:T(4,128)(2,1)S(1)}, bf16[4,2048]{1,0:T(4,128)(2,1)S(1)}, u32[]{:S(2)}, u32[]{:S(2)}) collective-permute-start(bf16[4,2048]{1,0:T(4,128)(2,1)S(1)} %get-tuple-element.29), channel_id=1, source_target_pairs={{1,0},{2,1},{3,2},{4,3},{5,4},{6,5},{7,6},{8,7},{9,8},{10,9},{11,1... | collective-permute-start | bytes 49160 | tf_op jit(solution)/shard_map/ppermute | solution.py:25
  24.2 113.5 %copy-start.4 = (bf16[64,2048]{1,0:T(8,128)(2,1)}, bf16[64,2048]{1,0:T(8,128)(2,1)S(1)}, u32[]{:S(2)}) copy-start(bf16[64,2048]{1,0:T(8,128)(2,1)S(1)} %convert_bitcast_fusion) | copy-start | bytes 786436
  28.4 18.7 %collective-permute-start.4 = (bf16[64,2048]{1,0:T(8,128)(2,1)S(1)}, bf16[64,2048]{1,0:T(8,128)(2,1)S(1)}, u32[]{:S(2)}, u32[]{:S(2)}) collective-permute-start(bf16[64,2048]{1,0:T(8,128)(2,1)S(1)} %fusion.90), channel_id=1, source_target_pairs={{0,32},{32,64},{64,96},{96,128},{128,160},{160,192},{192,224},{1,3... | collective-permute-start | bytes 786440 | tf_op jit(solution)/shard_map/ppermute | solution.py:33
  47.0 54.3 %copy-start.5 = (bf16[64,2048]{1,0:T(8,128)(2,1)}, bf16[64,2048]{1,0:T(8,128)(2,1)S(1)}, u32[]{:S(2)}) copy-start(bf16[64,2048]{1,0:T(8,128)(2,1)S(1)} %collective-permute-done.4) | copy-start | bytes 786436
  101.4 162.1 %all-gather.8.cloned.1.call-start = ((), (), s32[]{:S(2)}) async-start(), calls=%async_computation.2 | async-start | bytes 8650752 | tf_op jit(solution)/shard_map/all_gather | solution.py:99
  101.4 38.1 %copy-start.6 = (bf16[64,2048]{1,0:T(8,128)(2,1)S(1)}, bf16[64,2048]{1,0:T(8,128)(2,1)}, u32[]{:S(2)}) copy-start(bf16[64,2048]{1,0:T(8,128)(2,1)} %copy-done.5) | copy-start | bytes 786436
  101.4 17.5 %collective-permute-start.5 = (bf16[64,2048]{1,0:T(8,128)(2,1)}, bf16[64,2048]{1,0:T(8,128)(2,1)S(1)}, u32[]{:S(2)}, u32[]{:S(2)}) collective-permute-start(bf16[64,2048]{1,0:T(8,128)(2,1)} %get-tuple-element.30), channel_id=1, source_target_pairs={{32,0},{64,32},{96,64},{128,96},{160,128},{192,160},{224,192},{33,... | collective-permute-start | bytes 786440 | tf_op jit(solution)/shard_map/ppermute | solution.py:33
  119.0 15.0 %collective-permute-start.6 = (bf16[4,2048]{1,0:T(4,128)(2,1)S(1)}, bf16[4,2048]{1,0:T(4,128)(2,1)S(1)}, u32[]{:S(2)}, u32[]{:S(2)}) collective-permute-start(bf16[4,2048]{1,0:T(4,128)(2,1)S(1)} %get-tuple-element.24), channel_id=1, source_target_pairs={{0,1},{1,2},{2,3},{3,4},{4,5},{5,6},{6,7},{7,8},{8,9},{9,10},{10,1... | collective-permute-start | bytes 49160 | tf_op jit(solution)/shard_map/ppermute | solution.py:24
  132.1 5.5 %collective-permute-start.7 = (bf16[4,2048]{1,0:T(4,128)(2,1)S(1)}, bf16[4,2048]{1,0:T(4,128)(2,1)S(1)}, u32[]{:S(2)}, u32[]{:S(2)}) collective-permute-start(bf16[4,2048]{1,0:T(4,128)(2,1)S(1)} %get-tuple-element.25), channel_id=1, source_target_pairs={{1,0},{2,1},{3,2},{4,3},{5,4},{6,5},{7,6},{8,7},{9,8},{10,9},{11,1... | collective-permute-start | bytes 49160 | tf_op jit(solution)/shard_map/ppermute | solution.py:25
  140.1 4.3 %collective-permute-start.8 = (bf16[4,2048]{1,0:T(4,128)(2,1)S(1)}, bf16[4,2048]{1,0:T(4,128)(2,1)S(1)}, u32[]{:S(2)}, u32[]{:S(2)}) collective-permute-start(bf16[4,2048]{1,0:T(4,128)(2,1)S(1)} %get-tuple-element.22), channel_id=1, source_target_pairs={{0,1},{1,2},{2,3},{3,4},{4,5},{5,6},{6,7},{7,8},{8,9},{9,10},{10,1... | collective-permute-start | bytes 49160 | tf_op jit(solution)/shard_map/ppermute | solution.py:24
  142.0 5.6 %collective-permute-start.9 = (bf16[4,2048]{1,0:T(4,128)(2,1)S(1)}, bf16[4,2048]{1,0:T(4,128)(2,1)S(1)}, u32[]{:S(2)}, u32[]{:S(2)}) collective-permute-start(bf16[4,2048]{1,0:T(4,128)(2,1)S(1)} %get-tuple-element.23), channel_id=1, source_target_pairs={{1,0},{2,1},{3,2},{4,3},{5,4},{6,5},{7,6},{8,7},{9,8},{10,9},{11,1... | collective-permute-start | bytes 49160 | tf_op jit(solution)/shard_map/ppermute | solution.py:25
  149.7 10.8 %collective-permute-start.10 = (bf16[64,2048]{1,0:T(8,128)(2,1)S(1)}, bf16[64,2048]{1,0:T(8,128)(2,1)}, u32[]{:S(2)}, u32[]{:S(2)}) collective-permute-start(bf16[64,2048]{1,0:T(8,128)(2,1)S(1)} %fusion.105), channel_id=1, source_target_pairs={{0,32},{32,64},{64,96},{96,128},{128,160},{160,192},{192,224},{1,3... | collective-permute-start | bytes 786440 | tf_op jit(solution)/shard_map/ppermute | solution.py:33
  188.5 39.1 %copy-start.7 = (f32[64,2048]{1,0:T(8,128)S(1)}, f32[64,2048]{1,0:T(8,128)}, u32[]{:S(2)}) copy-start(f32[64,2048]{1,0:T(8,128)} %get-tuple-element.33) | copy-start | bytes 1572868
  188.6 17.1 %collective-permute-start.11 = (bf16[64,2048]{1,0:T(8,128)(2,1)}, bf16[64,2048]{1,0:T(8,128)(2,1)S(1)}, u32[]{:S(2)}, u32[]{:S(2)}) collective-permute-start(bf16[64,2048]{1,0:T(8,128)(2,1)} %get-tuple-element.32), channel_id=1, source_target_pairs={{32,0},{64,32},{96,64},{128,96},{160,128},{192,160},{224,192},{33,... | collective-permute-start | bytes 786440 | tf_op jit(solution)/shard_map/ppermute | solution.py:33
  205.7 15.4 %collective-permute-start.12 = (bf16[4,2048]{1,0:T(4,128)(2,1)S(1)}, bf16[4,2048]{1,0:T(4,128)(2,1)S(1)}, u32[]{:S(2)}, u32[]{:S(2)}) collective-permute-start(bf16[4,2048]{1,0:T(4,128)(2,1)S(1)} %get-tuple-element.20), channel_id=1, source_target_pairs={{0,1},{1,2},{2,3},{3,4},{4,5},{5,6},{6,7},{7,8},{8,9},{9,10},{10,1... | collective-permute-start | bytes 49160 | tf_op jit(solution)/shard_map/ppermute | solution.py:24
  219.2 5.6 %collective-permute-start.13 = (bf16[4,2048]{1,0:T(4,128)(2,1)S(1)}, bf16[4,2048]{1,0:T(4,128)(2,1)S(1)}, u32[]{:S(2)}, u32[]{:S(2)}) collective-permute-start(bf16[4,2048]{1,0:T(4,128)(2,1)S(1)} %get-tuple-element.21), channel_id=1, source_target_pairs={{1,0},{2,1},{3,2},{4,3},{5,4},{6,5},{7,6},{8,7},{9,8},{10,9},{11,1... | collective-permute-start | bytes 49160 | tf_op jit(solution)/shard_map/ppermute | solution.py:25
  229.0 4.3 %collective-permute-start.14 = (bf16[4,2048]{1,0:T(4,128)(2,1)S(1)}, bf16[4,2048]{1,0:T(4,128)(2,1)S(1)}, u32[]{:S(2)}, u32[]{:S(2)}) collective-permute-start(bf16[4,2048]{1,0:T(4,128)(2,1)S(1)} %get-tuple-element.18), channel_id=1, source_target_pairs={{0,1},{1,2},{2,3},{3,4},{4,5},{5,6},{6,7},{7,8},{8,9},{9,10},{10,1... | collective-permute-start | bytes 49160 | tf_op jit(solution)/shard_map/ppermute | solution.py:24
  230.9 5.6 %collective-permute-start.15 = (bf16[4,2048]{1,0:T(4,128)(2,1)S(1)}, bf16[4,2048]{1,0:T(4,128)(2,1)S(1)}, u32[]{:S(2)}, u32[]{:S(2)}) collective-permute-start(bf16[4,2048]{1,0:T(4,128)(2,1)S(1)} %get-tuple-element.19), channel_id=1, source_target_pairs={{1,0},{2,1},{3,2},{4,3},{5,4},{6,5},{7,6},{8,7},{9,8},{10,9},{11,1... | collective-permute-start | bytes 49160 | tf_op jit(solution)/shard_map/ppermute | solution.py:25
  238.5 36.4 %copy-start.8 = (f32[64,2048]{1,0:T(8,128)S(1)}, f32[64,2048]{1,0:T(8,128)}, u32[]{:S(2)}) copy-start(f32[64,2048]{1,0:T(8,128)} %get-tuple-element.3) | copy-start | bytes 1572868
  238.5 36.4 %collective-permute-start.16 = (bf16[64,2048]{1,0:T(8,128)(2,1)S(1)}, bf16[64,2048]{1,0:T(8,128)(2,1)S(1)}, u32[]{:S(2)}, u32[]{:S(2)}) collective-permute-start(bf16[64,2048]{1,0:T(8,128)(2,1)S(1)} %fusion.118), channel_id=1, source_target_pairs={{0,32},{32,64},{64,96},{96,128},{128,160},{160,192},{192,224},{1,3... | collective-permute-start | bytes 786440 | tf_op jit(solution)/shard_map/ppermute | solution.py:33
Sparse Core Ops, SparseCore 0:
  10.4 81.2 all-gather.3
  101.5 74.7 all-gather.5
  188.7 74.7 all-gather.7
where the time goes:
time: 283 us; the launch traced here: 282 us
  waiting for transfers between devices  148 us (52%)
  starting transfers between devices  67.8 us (24%)
  matrix products  33.1 us (12%)
  other arithmetic  18.6 us (7%)
  between operations  14.2 us (5%)
    all_gather x3, waiting for transfers between devices, correlate(): north_half = add_rows(lax.all_gather(lowered, 'strip', axis=0, tiled=True))  83.3 us
    ppermute x5, waiting for transfers between devices, shifted(): lax.ppermute(value, axis, [(source, source + steps) for source in range(l...  49.5 us
    ppermute x6, starting transfers between devices, with_halo(): before = lax.ppermute(last, axis, up)  38.1 us
    dot_general x3, matrix products, correlate(): jnp.dot(north_half.astype(jnp.bfloat16), east_corr, preferred_element_typ...  33.1 us
    ppermute x5, starting transfers between devices, shifted(): lax.ppermute(value, axis, [(source, source + steps) for source in range(l...  16.9 us
    ppermute x6, waiting for transfers between devices, with_halo(): after = lax.ppermute(leading, axis, down)  15.3 us
    ppermute x6, starting transfers between devices, with_halo(): after = lax.ppermute(leading, axis, down)  12.6 us
  transfers between devices with their start and end apart: 20, of which 12 were waited for; matrix products, arithmetic and copies ran while one was open for 10% of the time, Pallas kernels for 0%

commit v1 on v0

v1 whole, which is shorter than its diff:
```python
import functools

import jax
import jax.numpy as jnp
from jax import lax
from jax.experimental import pallas as pl
from jax.experimental.pallas import tpu as pltpu
from jax.sharding import PartitionSpec as P

STEPS = 4
ITERS = 2
PHASES = ITERS + 1
MESH = pl.DeviceIdType.MESH
F32, BF16 = jnp.float32, jnp.bfloat16

ROWS, WIDE, CHUNKS, LANES = 64, 80, 16, 128
HALO = 8
GATHER_PARTS = ((0, 1024, "zy"), (1024, 1024, "yz"))

DIFF, INCR, MULT = 0, 1, 2


def kernel(forcing, mult_in, incr_in, diff_in, north, east, mult_out, grad_out,
           north_all, east_all, low_land, half_land, half_mine, strip_land, rim_land, strip_mine, rim_mine,
           work, diff_prev, diff_own, incr_prev, incr_own, mult, force, half_flat, model,
           load_sem, gather_send, gather_recv, there_send, there_recv, core_sem, back_send, back_recv,
           swap_send, swap_recv, out_sem):
    sub, strip = lax.axis_index("sub"), lax.axis_index("strip")
    x, z_hi = lax.rem(sub, 4), lax.div(sub, 4)
    y, z, core = lax.div(strip, 8), lax.rem(lax.div(strip, 2), 4), lax.rem(strip, 2)
    chip, z_all = y * 4 + z, z_hi * 4 + z

    def device(x_at, y_at, z_at):
        return (lax.div(z_at, 4) * 4 + x_at, y_at * 8 + lax.rem(z_at, 4) * 2 + core)

    def along(dim, step):
        if dim == "y":
            return device(x, lax.rem(y + step + 4, 4), z_all)
        return device(x, y, lax.rem(z_all + step + 8, 8))

    peer = (sub, strip + 1 - 2 * core)

    def plane(offset):
        to = lax.rem(chip + offset, 16)
        return to, (sub, to * 2 + core)

    def remote(src, dst, send, recv, to):
        return pltpu.make_async_remote_copy(
            src_ref=src, dst_ref=dst, send_sem=send, recv_sem=recv, device_id=to, device_id_type=MESH
        )

    first, last = sub == 0, sub == 7
    top, bottom = strip == 0, strip == 31

    def load(source, target, sem):
        for j in range(CHUNKS):
            pltpu.make_async_copy(source.at[:, pl.ds(LANES * j, LANES)], target.at[j], sem).start()

    def loaded(target, sem):
        pltpu.make_async_copy(target, target, sem).wait()

    load(mult_in.at[0], mult, load_sem.at[0])
    load(incr_in.at[0], incr_own, load_sem.at[1])
    load(diff_in.at[0], force, load_sem.at[2])
    own_north = pltpu.make_async_copy(north, north_all.at[chip], load_sem.at[3])
    own_north.start()
    own_east = pltpu.make_async_copy(east, east_all, load_sem.at[4])
    own_east.start()
    rim_land[...] = jnp.zeros_like(rim_land)
    for ref in (work, diff_prev, diff_own):
        ref[0] = jnp.zeros((WIDE, LANES), F32)
        ref[CHUNKS + 1] = jnp.zeros((WIDE, LANES), F32)

    barrier = pltpu.get_barrier_semaphore()

    def greet(to):
        pl.semaphore_signal(barrier, inc=1, device_id=to, device_id_type=MESH)

    @pl.loop(1, 16)
    def _(offset):
        greet(plane(offset)[1])

    greet(peer)
    for step in (-1, 1):
        greet(along("z", step))
    near = [
        (-1, 0, ~first), (1, 0, ~last),
        (-1, -1, ~first & ~top), (-1, 1, ~first & ~bottom),
        (1, -1, ~last & ~top), (1, 1, ~last & ~bottom),
        (0, -1, ~top), (0, 1, ~bottom),
    ]
    for d_sub, d_strip, there in near:
        @pl.when(there)
        def _(d_sub=d_sub, d_strip=d_strip):
            greet((sub + d_sub, strip + d_strip))
    expected = 18
    for _, _, there in near:
        expected = expected + there.astype(jnp.int32)
    pl.semaphore_wait(barrier, expected)

    gather_sends = []

    def part_copy(part, piece, half, src, to, recv_at, sends):
        start, size, _ = GATHER_PARTS[part]
        if half is not None:
            start, size = start + half * (size // 2), size // 2
        columns = pl.ds(start, size)
        source = (north if src else north_all.at[piece]).at[:, columns]
        return remote(source, north_all.at[piece, :, columns], gather_send.at[sends], gather_recv.at[recv_at], to)

    def slot(part, rel_a, rel_b, half=0):
        return ((part * 4 + rel_a) * 4 + rel_b) * 2 + half

    def piece_of(part, rel_a, rel_b):
        rel_z, rel_y = (rel_a, rel_b) if GATHER_PARTS[part][2] == "zy" else (rel_b, rel_a)
        return lax.rem(y + rel_y, 4) * 4 + lax.rem(z + rel_z, 4)

    def gather_send_piece(part, rel_a, rel_b, dim_at, step, half=None):
        dim = GATHER_PARTS[part][2][dim_at]
        to_a, to_b = (rel_a, rel_b)
        if dim_at == 0:
            to_a = (rel_a - step) % 4
        else:
            to_b = (rel_b - step) % 4
        copy = part_copy(
            part, piece_of(part, rel_a, rel_b), half, (rel_a, rel_b) == (0, 0), along(dim, step),
            slot(part, to_a, to_b, half or 0), len(gather_sends),
        )
        copy.start()
        gather_sends.append(copy)

    def gather_wait(part, rel_a, rel_b, half=None):
        part_copy(part, piece_of(part, rel_a, rel_b), half, False, peer, slot(part, rel_a, rel_b, half or 0), 0).wait_recv()

    parts = range(len(GATHER_PARTS))
    for part in parts:
        for dim_at in (0, 1):
            for step in (1, -1):
                gather_send_piece(part, 0, 0, dim_at, step)

    def gather_first_ring():
        for rel, step in ((3, 1), (1, -1)):
            for part in parts:
                gather_wait(part, rel, 0)
                gather_send_piece(part, rel, 0, 0, step, half=0 if step == 1 else 1)
                gather_send_piece(part, rel, 0, 1, 1)
                gather_send_piece(part, rel, 0, 1, -1)

    def gather_own_second():
        for rel, step in ((3, 1), (1, -1)):
            for part in parts:
                gather_wait(part, 0, rel)
                gather_send_piece(part, 0, rel, 1, step, half=0 if step == 1 else 1)

    def gather_far():
        for part in parts:
            gather_wait(part, 2, 0, 0)
            gather_wait(part, 2, 0, 1)
            gather_send_piece(part, 2, 0, 1, 1)
            gather_send_piece(part, 2, 0, 1, -1)

    def gather_rest():
        for rel_a in (3, 1, 2):
            for rel, step in ((3, 1), (1, -1)):
                for part in parts:
                    gather_wait(part, rel_a, rel)
                    gather_send_piece(part, rel_a, rel, 1, step, half=0 if step == 1 else 1)
        for rel_a in (0, 3, 1, 2):
            for part in parts:
                gather_wait(part, rel_a, 2, 0)
                gather_wait(part, rel_a, 2, 1)

    def swap_copies(which):
        copies = []
        for at, d_sub in ((0, 1), (1, -1)):
            if which < MULT and d_sub == -1:
                continue
            sent = ~last if d_sub == 1 else ~first
            heard = ~first if d_sub == 1 else ~last
            copies.append((remote(
                strip_mine.at[which], strip_land.at[which, at], swap_send.at[which, at],
                swap_recv.at[which, at], (sub + d_sub, strip)), sent, heard))
        for at, d_sub in ((0, 1), (1, 0), (2, -1)):
            if (which == INCR and d_sub == 0) or (which < MULT and d_sub == -1):
                continue
            sub_sent = {1: ~last, 0: first | ~first, -1: ~first}[d_sub]
            sub_heard = {1: ~first, 0: first | ~first, -1: ~last}[d_sub]
            for edge, d_strip in ((0, -1), (1, 1)):
                sent = sub_sent & (~top if d_strip == -1 else ~bottom)
                heard = sub_heard & (~bottom if d_strip == -1 else ~top)
                number = 2 + 2 * at + edge
                copies.append((remote(
                    rim_mine.at[which, edge], rim_land.at[which, at, 1 - edge], swap_send.at[which, number],
                    swap_recv.at[which, number], (sub + d_sub, strip + d_strip)), sent, heard))
        return copies

    def swap_start(which):
        for copy, sent, _ in swap_copies(which):
            pl.when(sent)(copy.start)

    def swap_wait(which, wanted):
        for copy, _, heard in swap_copies(which):
            if wanted(copy):
                pl.when(heard)(copy.wait_recv)

    def swap_wait_number(which, numbers):
        copies = swap_copies(which)
        order = ([0, 1] if which >= MULT else [0]) + [
            2 + 2 * at + edge
            for at, d_sub in ((0, 1), (1, 0), (2, -1))
            if not ((which == INCR and d_sub == 0) or (which < MULT and d_sub == -1))
            for edge in (0, 1)
        ]
        for number, (copy, _, heard) in zip(order, copies, strict=True):
            if number in numbers:
                pl.when(heard)(copy.wait_recv)

    FROM_BEFORE, FROM_SAME, FROM_AFTER = (0, 2, 3), (4, 5), (1, 6, 7)

    def pack(which, field):
        @pl.loop(0, CHUNKS // 2)
        def _(pair):
            left, right = field[2 * pair], field[2 * pair + 1]
            strip_mine[which, 2 * pair] = left.astype(BF16)
            strip_mine[which, 2 * pair + 1] = right.astype(BF16)
            rim_mine[which, 0, pair] = jnp.concatenate([left[:HALO], right[:HALO]], axis=0).astype(BF16)
            rim_mine[which, 1, pair] = jnp.concatenate([left[-HALO:], right[-HALO:]], axis=0).astype(BF16)

    def widened(which, source, chunk_rows, pair):
        above = rim_land[which, source, 0, pair].astype(F32)
        below = rim_land[which, source, 1, pair].astype(F32)
        return [
            jnp.concatenate(
                [above[h * HALO:(h + 1) * HALO], chunk_rows(2 * pair + h), below[h * HALO:(h + 1) * HALO]], axis=0
            )
            for h in (0, 1)
        ]

    def each_wide(which, source, chunk_rows, put):
        @pl.loop(0, CHUNKS // 2)
        def _(pair):
            for h, value in enumerate(widened(which, source, chunk_rows, pair)):
                put(2 * pair + h, value)

    def landed(which, source):
        return lambda j: strip_land[which, source, j].astype(F32)

    lane = lax.broadcasted_iota(jnp.int32, (WIDE, LANES), 1)
    leftmost, rightmost = lane == 0, lane == LANES - 1

    def spread(before, now, now_left, after_left):
        now_right = pltpu.roll(now, 1, 1)
        total = (
            jnp.where(leftmost, before, now_right) + jnp.where(rightmost, after_left, now_left)
            + pltpu.roll(now, 1, 0) + pltpu.roll(now, WIDE - 1, 0) - 4.0 * now
        )
        return total, now_right

    def run_model(diff):
        @pl.loop(0, STEPS)
        def _(step):
            def body(j, carry):
                before, now, now_left = carry
                after = work[j + 1]
                after_left = pltpu.roll(after, LANES - 1, 1)
                total, now_right = spread(before, now, now_left, after_left)
                work[j] = now + diff[j] * total
                return now_right, after, after_left
            start = work[1]
            lax.fori_loop(1, CHUNKS + 1, body, (jnp.zeros((WIDE, LANES), F32), start, pltpu.roll(start, LANES - 1, 1)))

    def run_adjoint(diff):
        @pl.loop(0, STEPS)
        def _(step):
            def body(j, carry):
                before, now, now_left, field = carry
                later = work[j + 1]
                after = diff[j + 1] * later
                after_left = pltpu.roll(after, LANES - 1, 1)
                total, now_right = spread(before, now, now_left, after_left)
                work[j] = field + total
                return now_right, after, after_left, later
            field = work[1]
            start = diff[1] * field
            lax.fori_loop(
                1, CHUNKS + 1, body, (jnp.zeros((WIDE, LANES), F32), start, pltpu.roll(start, LANES - 1, 1), field)
            )

    def put_work(j, value):
        work[j + 1] = value

    row = lax.broadcasted_iota(jnp.int32, (WIDE, LANES), 0)
    inside = ~((row < HALO) & top) & ~((row >= HALO + ROWS) & bottom)

    def there_copy(phase, offset):
        to, at = plane(offset)
        return remote(
            strip_mine.at[MULT - 1 + phase if phase else 4, to], low_land.at[phase, chip, core],
            there_send.at[phase, offset], there_recv.at[phase, offset], at)

    def there_start(phase):
        @pl.loop(1, 16)
        def _(offset):
            there_copy(phase, offset).start()
        low_land[phase, chip, core] = strip_mine[MULT - 1 + phase if phase else 4, chip]

    def core_copy(phase):
        mine = low_land.at[phase, :, core]
        return remote(mine, mine, core_sem.at[phase, 0], core_sem.at[phase, 1], peer)

    def there_wait(phase):
        @pl.loop(1, 16)
        def _(offset):
            there_copy(phase, offset).wait_recv()
        core_copy(phase).start()

    def back_copy(phase, offset):
        to, at = plane(offset)
        return remote(
            half_mine.at[phase, to], half_land.at[phase, chip], back_send.at[phase, offset],
            back_recv.at[phase, offset], at)

    def north_product(phase):
        core_copy(phase).wait_recv()

        @pl.loop(0, 4)
        def _(quarter):
            blocks = north_all[pl.ds(4 * quarter, 4)].reshape(4 * ROWS, 2048)
            columns = low_land[phase].reshape(2048, LANES)
            product = jnp.dot(blocks, columns, preferred_element_type=F32).astype(BF16)
            half_mine[phase, pl.ds(4 * quarter, 4)] = product.reshape(4, ROWS, LANES)

        @pl.loop(1, 16)
        def _(offset):
            back_copy(phase, offset).start()
        half_land[phase, chip] = half_mine[phase, chip]

    def east_product(phase, finish):
        @pl.loop(1, 16)
        def _(offset):
            back_copy(phase, offset).wait_recv()
        for j in range(CHUNKS):
            half_flat[:, LANES * j:LANES * (j + 1)] = half_land[phase, j]

        @pl.loop(0, 8)
        def _(pair):
            columns = pl.ds(pl.multiple_of(256 * pair, 256), 256)
            product = jnp.dot(half_flat[...], east_all[:, columns], preferred_element_type=F32)
            finish(2 * pair, product[:, :LANES])
            finish(2 * pair + 1, product[:, LANES:])

    loaded(mult, load_sem.at[0])

    @pl.loop(0, CHUNKS)
    def _(j):
        strip_mine[4, j] = mult[j].astype(BF16)

    there_start(0)
    loaded(force, load_sem.at[2])
    pack(DIFF, force)
    swap_start(DIFF)
    loaded(incr_own, load_sem.at[1])
    pack(INCR, incr_own)
    swap_start(INCR)
    gather_first_ring()
    gather_own_second()
    gather_far()
    there_wait(0)
    swap_wait_number(DIFF, FROM_SAME)

    def put_own(j, value):
        diff_own[j + 1] = value

    each_wide(DIFF, 1, lambda j: force[j], put_own)
    load(forcing.at[0], force, load_sem.at[2])
    swap_wait_number(DIFF, FROM_BEFORE)

    def put_prev(j, value):
        diff_prev[j + 1] = value

    each_wide(DIFF, 0, landed(DIFF, 0), put_prev)
    swap_wait_number(INCR, FROM_BEFORE)

    def put_incr(j, value):
        incr_prev[j] = value
        work[j + 1] = value

    each_wide(INCR, 0, landed(INCR, 0), put_incr)
    own_north.wait()
    gather_rest()
    north_product(0)
    run_model(diff_prev)

    def keep_model():
        @pl.loop(0, CHUNKS)
        def _(j):
            moved = jnp.where(first, 0.0, work[j + 1, HALO:HALO + ROWS])
            model[j] = force[j] - incr_own[j] + moved

    loaded(force, load_sem.at[2])
    keep_model()
    own_east.wait()

    def update(j, product):
        mult[j] = mult[j] + 0.5 * (model[j] - product)

    east_product(0, update)

    for phase in range(1, PHASES):
        which = MULT - 1 + phase
        final = phase == PHASES - 1
        pack(which, mult)
        there_start(phase)
        swap_start(which)
        swap_wait_number(which, FROM_SAME)
        each_wide(which, 1, lambda j: mult[j], put_work)
        run_adjoint(diff_prev)
        there_wait(phase)

        @pl.loop(0, CHUNKS)
        def _(j):
            incr_prev[j] = incr_prev[j] - 0.5 * work[j + 1]

        north_product(phase)
        swap_wait_number(which, FROM_BEFORE)

        def put_before(j, value):
            value = jnp.where(inside, incr_prev[j] + 0.5 * value, 0.0)
            incr_prev[j] = value
            work[j + 1] = value

        each_wide(which, 0, landed(which, 0), put_before)
        run_model(diff_prev)

        @pl.loop(0, CHUNKS)
        def _(j):
            model[j] = force[j] + jnp.where(first, 0.0, work[j + 1, HALO:HALO + ROWS])

        swap_wait_number(which, FROM_AFTER)
        each_wide(which, 2, landed(which, 1), put_work)
        run_adjoint(diff_own)

        @pl.loop(0, CHUNKS)
        def _(j):
            grad = mult[j] - jnp.where(last, 0.0, work[j + 1, HALO:HALO + ROWS])
            incr = incr_own[j] + 0.5 * grad
            incr_own[j] = incr
            model[j] = model[j] - incr
            if final:
                work[j + 1, HALO:HALO + ROWS] = grad

        def stored(source, target, sem):
            return [
                pltpu.make_async_copy(source(j), target.at[0, :, pl.ds(LANES * j, LANES)], sem) for j in range(CHUNKS)
            ]

        if not final:
            east_product(phase, update)
        else:
            for copy in stored(lambda j: work.at[j + 1, pl.ds(HALO, ROWS)], grad_out, out_sem.at[0]):
                copy.start()

            def finish(j, product):
                model[j] = model[j] - product

            east_product(phase, finish)
            for copy in stored(lambda j: model.at[j], mult_out, out_sem.at[1]):
                copy.start()

    for copy in gather_sends:
        copy.wait_send()
    for phase in range(PHASES):
        @pl.loop(1, 16)
        def _(offset, phase=phase):
            there_copy(phase, offset).wait_send()
            back_copy(phase, offset).wait_send()
        core_copy(phase).wait_send()
    for which in (DIFF, INCR, MULT, MULT + 1):
        for copy, sent, _ in swap_copies(which):
            pl.when(sent)(copy.wait_send)
    pltpu.make_async_copy(model, model, out_sem.at[0]).wait()
    pltpu.make_async_copy(model, model, out_sem.at[1]).wait()


def local(forcing, mult_start, incr_start, diffusivity, north_corr, east_corr):
    any_space = pl.BlockSpec(memory_space=pl.ANY)
    dma = pltpu.SemaphoreType.DMA
    strip = (CHUNKS, ROWS, LANES)
    wide = (CHUNKS, WIDE, LANES)
    padded = (CHUNKS + 2, WIDE, LANES)
    pieces = len(GATHER_PARTS)
    out = jax.ShapeDtypeStruct((1, ROWS, 2048), F32)
    return pl.pallas_call(
        kernel,
        out_shape=(out, out),
        in_specs=[any_space] * 6,
        out_specs=(any_space, any_space),
        scratch_shapes=[
            pltpu.VMEM((16, ROWS, 2048), BF16),
            pltpu.VMEM((2048, 2048), BF16),
            pltpu.VMEM((PHASES, 16, 2, ROWS, LANES), BF16),
            pltpu.VMEM((PHASES,) + strip, BF16),
            pltpu.VMEM((PHASES,) + strip, BF16),
            pltpu.VMEM((4, 2) + strip, BF16),
            pltpu.VMEM((4, 3, 2, CHUNKS // 2, 2 * HALO, LANES), BF16),
            pltpu.VMEM((5,) + strip, BF16),
            pltpu.VMEM((4, 2, CHUNKS // 2, 2 * HALO, LANES), BF16),
            pltpu.VMEM(padded, F32),
            pltpu.VMEM(padded, F32),
            pltpu.VMEM(padded, F32),
            pltpu.VMEM(wide, F32),
            pltpu.VMEM(strip, F32),
            pltpu.VMEM(strip, F32),
            pltpu.VMEM(strip, F32),
            pltpu.VMEM((ROWS, 2048), BF16),
            pltpu.VMEM(strip, F32),
            dma((5,)),
            dma((pieces * 20,)),
            dma((pieces * 32,)),
            dma((PHASES, 16)),
            dma((PHASES, 16)),
            dma((PHASES, 2)),
            dma((PHASES, 16)),
            dma((PHASES, 16)),
            dma((4, 8)),
            dma((4, 8)),
            dma((2,)),
        ],
        compiler_params=pltpu.CompilerParams(
            collective_id=0, has_side_effects=True, vmem_limit_bytes=48 * 2**20
        ),
    )(forcing, mult_start, incr_start, diffusivity, north_corr, east_corr)


def solution(mesh):
    rows = P("sub", "strip", None)
    return jax.shard_map(
        local,
        mesh=mesh,
        in_specs=(rows, rows, rows, rows, P("strip", None), P()),
        out_specs=(rows, rows),
        check_vma=False,
    )
```

time: 283 us -> 172 us (0.61)
  Pallas kernels: 0 us -> 164 us
  waiting for transfers between devices: 148 us -> 0 us
  starting transfers between devices: 67.8 us -> 0 us
  matrix products: 33.1 us -> 0 us
  other arithmetic: 18.6 us -> 0 us
  between operations: 14.2 us -> 0.65 us
  local copies, waits for them, and re-layouts: 0.44 us -> 6.7 us
    pallas_call x0 -> x1, Pallas kernels: none -> 164 us  [local(): pl.pallas_call(kernel, out_shape=(out, out), in_specs=[any_space] * 6, ou...]
    all_gather x3 -> x0, waiting for transfers between devices: 83.3 us -> none  [correlate(): north_half = add_rows(lax.all_gather(lowered, 'strip', axis=0, tiled=True))]
    ppermute x17 -> x0, starting transfers between devices: 67.6 us -> none  [the longest x6 38.1 us: with_halo(): before = lax.ppermute(last, axis, up)]
    ppermute x17 -> x0, waiting for transfers between devices: 64.8 us -> none  [the longest x5 49.5 us: shifted(): lax.ppermute(value, axis, [(source, source + steps) for source in range(l...]
    dot_general x3 -> x0, matrix products: 33.1 us -> none  [correlate(): jnp.dot(north_half.astype(jnp.bfloat16), east_corr, preferred_element_typ...]
    mul x17 -> x0, other arithmetic: 9.02 us -> none  [the longest x8 4.68 us: adjoint(): weighted = diffuse_wide[each_step:each_step + widened.shape[0]] * widened]
    convert_element_type x16 -> x0, other arithmetic: 8.7 us -> none  [the longest x6 4.28 us: shortened(): a.astype(jnp.bfloat16)]
    unnamed x18 -> x12, local copies, waits for them, and re-layouts: 0.05 us -> 6.7 us
  transfers between devices with their start and end apart: 20 -> 0, of which waited for: 12 -> 0; matrix products, arithmetic and copies ran while one was open for 10% -> 0% of each run, Pallas kernels for 0% -> 0%
where the time goes in v1:
time: 172 us; the launch traced here: 171 us
  Pallas kernels  164 us (95%)
  local copies, waits for them, and re-layouts  6.7 us (4%)
    pallas_call x1, Pallas kernels, local(): pl.pallas_call(kernel, out_shape=(out, out), in_specs=[any_space] * 6, ou...  164 us
    unnamed x12, local copies, waits for them, and re-layouts  6.7 us

profile of v1, /device:TPU:7, one launch (start us, length us, event | category | flops | bytes accessed | tf_op | source)
XLA Modules:
  0.0 171.1 jit_solution(14157342850474665165)
XLA Ops:
  0.6 0.0 copy-start
  0.6 1.0 copy-done
  1.7 0.0 copy-start.1
  1.7 1.0 copy-done.1
  2.7 0.0 copy-start.2
  2.7 1.0 copy-done.2
  3.8 0.0 copy-start.3
  3.8 1.0 copy-done.3
  4.8 0.0 copy-start.4
  4.8 0.9 copy-done.4
  5.8 163.8 %shard_map.77 = (f32[1,64,2048]{2,1,0:T(8,128)S(1)}, f32[1,64,2048]{2,1,0:T(8,128)S(1)}) custom-call(f32[1,64,2048]{2,1,0:T(8,128)S(1)} %copy-done, f32[1,64,2048]{2,1,0:T(8,128)S(1)} %copy-done.1, f32[1,64,2048]{2,1,0:T(8,128)S(1)} %copy-done.2, f32[1,64,2048]{2,1,0:T(8,128)S(1)} %copy-done.3, bf16[64,2048]{1,0:T(8,128)(2,1)S(1)} %copy-done.4, ...), custom_call_target="tpu_custom_call" | custom-call | tf_op jit(solution)/shard_map/pallas_call | solution.py:493
  169.5 0.8 copy.10
  170.3 0.8 copy.11
Async XLA Ops:
  0.6 1.0 copy-start
  1.7 1.0 copy-start.1
  2.7 1.0 copy-start.2
  3.8 1.0 copy-start.3
  4.8 0.9 copy-start.4

commit v2 on v1

--- a/solution.py
+++ b/solution.py
@@ -22,9 +22,9 @@
 
 def kernel(forcing, mult_in, incr_in, diff_in, north, east, mult_out, grad_out,
            north_all, east_all, low_land, half_land, half_mine, strip_land, rim_land, strip_mine, rim_mine,
-           work, diff_prev, diff_own, incr_prev, incr_own, mult, force, half_flat, model,
-           load_sem, gather_send, gather_recv, there_send, there_recv, core_sem, back_send, back_recv,
-           swap_send, swap_recv, out_sem):
+           work, diff_prev, diff_own, incr_prev, incr_own, mult, force, model, north_sum, east_sum, relay_out, relay_in,
+           load_sem, gather_send, gather_recv, there_send, there_recv, core_send, core_recv, back_send, back_recv,
+           swap_send, swap_recv, relay_send, relay_recv, out_sem):
     sub, strip = lax.axis_index("sub"), lax.axis_index("strip")
     x, z_hi = lax.rem(sub, 4), lax.div(sub, 4)
     y, z, core = lax.div(strip, 8), lax.rem(lax.div(strip, 2), 4), lax.rem(strip, 2)
@@ -51,6 +51,9 @@
 
     first, last = sub == 0, sub == 7
     top, bottom = strip == 0, strip == 31
+    hub = jnp.where(z_hi == 0, 3, 4)
+    is_hub = sub == hub
+    across = (lax.rem(sub + 4, 8), strip)
 
     def load(source, target, sem):
         for j in range(CHUNKS):
@@ -76,11 +79,10 @@
     def greet(to):
         pl.semaphore_signal(barrier, inc=1, device_id=to, device_id_type=MESH)
 
-    @pl.loop(1, 16)
-    def _(offset):
+    for offset in range(1, 16):
         greet(plane(offset)[1])
-
     greet(peer)
+    greet(across)
     for step in (-1, 1):
         greet(along("z", step))
     near = [
@@ -93,7 +95,16 @@
         @pl.when(there)
         def _(d_sub=d_sub, d_strip=d_strip):
             greet((sub + d_sub, strip + d_strip))
-    expected = 18
+    for part in range(4):
+        @pl.when(is_hub & (x != part))
+        def _(part=part):
+            greet((z_hi * 4 + part, strip))
+
+    @pl.when(~is_hub)
+    def _():
+        greet((hub, strip))
+
+    expected = 19 + jnp.where(is_hub, 3, 1)
     for _, _, there in near:
         expected = expected + there.astype(jnp.int32)
     pl.semaphore_wait(barrier, expected)
@@ -175,8 +186,8 @@
         for at, d_sub in ((0, 1), (1, -1)):
             if which < MULT and d_sub == -1:
                 continue
-            sent = ~last if d_sub == 1 else ~first
-            heard = ~first if d_sub == 1 else ~last
+            sent = ~last & (sub != 3) if d_sub == 1 else ~first & (sub != 4)
+            heard = ~first & (sub != 4) if d_sub == 1 else ~last & (sub != 3)
             copies.append((remote(
                 strip_mine.at[which], strip_land.at[which, at], swap_send.at[which, at],
                 swap_recv.at[which, at], (sub + d_sub, strip)), sent, heard))
@@ -195,13 +206,9 @@
         return copies
 
     def swap_start(which):
+        relay_from_hub(which)
         for copy, sent, _ in swap_copies(which):
             pl.when(sent)(copy.start)
-
-    def swap_wait(which, wanted):
-        for copy, _, heard in swap_copies(which):
-            if wanted(copy):
-                pl.when(heard)(copy.wait_recv)
 
     def swap_wait_number(which, numbers):
         copies = swap_copies(which)
@@ -215,14 +222,79 @@
             if number in numbers:
                 pl.when(heard)(copy.wait_recv)
 
+    def relay_copies(which):
+        up_only = which < MULT
+        gives = z_hi == 0 if up_only else z_hi >= 0
+        takes = z_hi == 1 if up_only else z_hi >= 0
+        land = 0 if up_only else jnp.where(z_hi == 0, 1, 0)
+        far_land = 0 if up_only else 1 - land
+        quarter = lambda ref, part: ref.at[pl.ds(4 * part, 4)]
+        send, recv = relay_send.at[which], relay_recv.at[which]
+        outward = [
+            (remote(quarter(strip_mine.at[which], part), relay_out.at[which], send.at[part], recv.at[0],
+                    (z_hi * 4 + part, strip)), gives & is_hub & (x != part))
+            for part in range(4)
+        ]
+        mine, kept = quarter(strip_mine.at[which], x), relay_out.at[which]
+        there, there_kept = quarter(strip_land.at[which, far_land], x), relay_in.at[which]
+        far_hub = across[0] == 7 - hub
+        over = [
+            (remote(mine, there_kept, send.at[4], recv.at[1], across), gives & is_hub),
+            (remote(kept, there, send.at[4], recv.at[1], across), gives & ~is_hub & far_hub),
+            (remote(kept, there_kept, send.at[4], recv.at[1], across), gives & ~is_hub & ~far_hub),
+        ]
+        inward = (remote(relay_in.at[which], quarter(strip_land.at[which, land], x), send.at[5], recv.at[2 + x], (hub, strip)),
+                  takes & ~is_hub)
+        waits = {
+            "out": (outward[0][0], gives & ~is_hub),
+            "over": (over[0][0], takes),
+            "in": [
+                (remote(relay_in.at[which], quarter(strip_land.at[which, land], part), send.at[5], recv.at[2 + part], (hub, strip)),
+                 takes & is_hub & (x != part))
+                for part in range(4)
+            ],
+        }
+        return outward, over, inward, waits
+
+    def relay_from_hub(which):
+        outward, over, _, _ = relay_copies(which)
+        pl.when(over[0][1])(over[0][0].start)
+        for copy, sent in outward:
+            pl.when(sent)(copy.start)
+
+    def relay_across(which):
+        _, over, _, waits = relay_copies(which)
+        copy, heard = waits["out"]
+        pl.when(heard)(copy.wait_recv)
+        for copy, sent in over[1:]:
+            pl.when(sent)(copy.start)
+
+    def relay_to_hub(which):
+        _, _, (copy, sent), waits = relay_copies(which)
+        arrived, heard = waits["over"]
+        pl.when(heard)(arrived.wait_recv)
+        pl.when(sent)(copy.start)
+
+    def relay_end(which, hub_sub):
+        for copy, heard in relay_copies(which)[3]["in"]:
+            pl.when(heard & (sub == hub_sub))(copy.wait_recv)
+
+    def relay_sent(which):
+        outward, over, (copy, sent), _ = relay_copies(which)
+        for one, was in outward:
+            pl.when(was)(one.wait_send)
+        gives = over[0][1] | over[1][1] | over[2][1]
+        pl.when(gives)(over[0][0].wait_send)
+        pl.when(sent)(copy.wait_send)
+
     FROM_BEFORE, FROM_SAME, FROM_AFTER = (0, 2, 3), (4, 5), (1, 6, 7)
 
     def pack(which, field):
-        @pl.loop(0, CHUNKS // 2)
-        def _(pair):
+        for pair in range(CHUNKS // 2):
             left, right = field[2 * pair], field[2 * pair + 1]
-            strip_mine[which, 2 * pair] = left.astype(BF16)
-            strip_mine[which, 2 * pair + 1] = right.astype(BF16)
+            if which < MULT:
+                strip_mine[which, 2 * pair] = left.astype(BF16)
+                strip_mine[which, 2 * pair + 1] = right.astype(BF16)
             rim_mine[which, 0, pair] = jnp.concatenate([left[:HALO], right[:HALO]], axis=0).astype(BF16)
             rim_mine[which, 1, pair] = jnp.concatenate([left[-HALO:], right[-HALO:]], axis=0).astype(BF16)
 
@@ -237,8 +309,7 @@
         ]
 
     def each_wide(which, source, chunk_rows, put):
-        @pl.loop(0, CHUNKS // 2)
-        def _(pair):
+        for pair in range(CHUNKS // 2):
             for h, value in enumerate(widened(which, source, chunk_rows, pair)):
                 put(2 * pair + h, value)
 
@@ -256,35 +327,23 @@
         )
         return total, now_right
 
-    def run_model(diff):
+    def run_steps(diff, adjoint):
+        nothing = jnp.zeros((WIDE, LANES), F32)
+
         @pl.loop(0, STEPS)
         def _(step):
-            def body(j, carry):
-                before, now, now_left = carry
-                after = work[j + 1]
-                after_left = pltpu.roll(after, LANES - 1, 1)
+            field = work[1]
+            before, now = nothing, diff[1] * field if adjoint else field
+            now_left = pltpu.roll(now, LANES - 1, 1)
+            for j in range(1, CHUNKS + 1):
+                later = after = after_left = nothing
+                if j < CHUNKS:
+                    later = work[j + 1]
+                    after = diff[j + 1] * later if adjoint else later
+                    after_left = pltpu.roll(after, LANES - 1, 1)
                 total, now_right = spread(before, now, now_left, after_left)
-                work[j] = now + diff[j] * total
-                return now_right, after, after_left
-            start = work[1]
-            lax.fori_loop(1, CHUNKS + 1, body, (jnp.zeros((WIDE, LANES), F32), start, pltpu.roll(start, LANES - 1, 1)))
-
-    def run_adjoint(diff):
-        @pl.loop(0, STEPS)
-        def _(step):
-            def body(j, carry):
-                before, now, now_left, field = carry
-                later = work[j + 1]
-                after = diff[j + 1] * later
-                after_left = pltpu.roll(after, LANES - 1, 1)
-                total, now_right = spread(before, now, now_left, after_left)
-                work[j] = field + total
-                return now_right, after, after_left, later
-            field = work[1]
-            start = diff[1] * field
-            lax.fori_loop(
-                1, CHUNKS + 1, body, (jnp.zeros((WIDE, LANES), F32), start, pltpu.roll(start, LANES - 1, 1), field)
-            )
+                work[j] = field + total if adjoint else now + diff[j] * total
+                before, now, now_left, field = now_right, after, after_left, later
 
     def put_work(j, value):
         work[j + 1] = value
@@ -292,70 +351,100 @@
     row = lax.broadcasted_iota(jnp.int32, (WIDE, LANES), 0)
     inside = ~((row < HALO) & top) & ~((row >= HALO + ROWS) & bottom)
 
-    def there_copy(phase, offset):
-        to, at = plane(offset)
-        return remote(
-            strip_mine.at[MULT - 1 + phase if phase else 4, to], low_land.at[phase, chip, core],
-            there_send.at[phase, offset], there_recv.at[phase, offset], at)
-
-    def there_start(phase):
-        @pl.loop(1, 16)
-        def _(offset):
-            there_copy(phase, offset).start()
-        low_land[phase, chip, core] = strip_mine[MULT - 1 + phase if phase else 4, chip]
-
-    def core_copy(phase):
-        mine = low_land.at[phase, :, core]
-        return remote(mine, mine, core_sem.at[phase, 0], core_sem.at[phase, 1], peer)
-
-    def there_wait(phase):
-        @pl.loop(1, 16)
-        def _(offset):
-            there_copy(phase, offset).wait_recv()
-        core_copy(phase).start()
-
-    def back_copy(phase, offset):
-        to, at = plane(offset)
-        return remote(
-            half_mine.at[phase, to], half_land.at[phase, chip], back_send.at[phase, offset],
-            back_recv.at[phase, offset], at)
+    low_of = (4, MULT, MULT + 1)
+
+    def chip_at(to):
+        return (sub, to * 2 + core)
+
+    def apart(low, high):
+        return lax.rem(high - low + 16, 16)
+
+    def there_copy(phase, to):
+        at = apart(chip, to)
+        return remote(strip_mine.at[low_of[phase], to], low_land.at[phase, chip, core],
+                      there_send.at[phase, at], there_recv.at[phase, at], chip_at(to))
+
+    def there_own(phase):
+        low_land[phase, chip, core] = strip_mine[low_of[phase], chip]
+
+    def core_copy(phase, row):
+        mine = low_land.at[phase, pl.ds(4 * row, 4), core]
+        at = lax.rem(row - y + 4, 4)
+        return remote(mine, mine, core_send.at[phase, at], core_recv.at[phase, at], peer)
+
+    def back_copy(phase, to):
+        at = apart(chip, to)
+        return remote(half_mine.at[phase, to], half_land.at[phase, chip],
+                      back_send.at[phase, at], back_recv.at[phase, at], chip_at(to))
+
+    def from_row(make, recv, phase, d_row):
+        row = lax.rem(y + d_row, 4)
+        for d_z in range(1 if d_row == 0 else 0, 4):
+            source = row * 4 + lax.rem(z + d_z, 4)
+            copy = make(phase, source)
+            at = apart(source, chip)
+            remote(copy.src_ref, copy.dst_ref, recv.at[phase, at], recv.at[phase, at], peer).wait_recv()
+        return row
+
+    ORDER = (0, 1, 3, 2)
 
     def north_product(phase):
-        core_copy(phase).wait_recv()
-
-        @pl.loop(0, 4)
-        def _(quarter):
-            blocks = north_all[pl.ds(4 * quarter, 4)].reshape(4 * ROWS, 2048)
-            columns = low_land[phase].reshape(2048, LANES)
-            product = jnp.dot(blocks, columns, preferred_element_type=F32).astype(BF16)
-            half_mine[phase, pl.ds(4 * quarter, 4)] = product.reshape(4, ROWS, LANES)
-
-        @pl.loop(1, 16)
-        def _(offset):
-            back_copy(phase, offset).start()
+        rows = []
+
+        def arrive(d_row):
+            row = from_row(there_copy, there_recv, phase, d_row)
+            core_copy(phase, row).start()
+            rows.append(row)
+
+        def columns(row):
+            return low_land[phase, pl.ds(4 * row, 4)].reshape(4 * 2 * ROWS, LANES)
+
+        arrive(ORDER[0])
+        for number in range(4):
+            if number < 3:
+                arrive(ORDER[number + 1])
+            row = rows[number]
+            core_copy(phase, row).wait_recv()
+            depth = pl.ds(pl.multiple_of(512 * row, 512), 512)
+            if number < 3:
+                product = jnp.dot(
+                    north_all[:, :, depth].reshape(1024, 512), columns(row), preferred_element_type=F32)
+                north_sum[...] = product if number == 0 else north_sum[...] + product
+                continue
+            for d_row in (2, 1, 3, 0):
+                to_row = lax.rem(y + d_row, 4)
+                part = pl.ds(pl.multiple_of(256 * to_row, 256), 256)
+                product = jnp.dot(
+                    north_all[pl.ds(4 * to_row, 4), :, depth].reshape(256, 512), columns(row),
+                    preferred_element_type=F32)
+                half = (north_sum[part, :] + product).astype(BF16).reshape(4, ROWS, LANES)
+                half_mine[phase, pl.ds(4 * to_row, 4)] = half
+                for d_z in range(1 if d_row == 0 else 0, 4):
+                    back_copy(phase, to_row * 4 + lax.rem(z + d_z, 4)).start()
         half_land[phase, chip] = half_mine[phase, chip]
 
     def east_product(phase, finish):
-        @pl.loop(1, 16)
-        def _(offset):
-            back_copy(phase, offset).wait_recv()
-        for j in range(CHUNKS):
-            half_flat[:, LANES * j:LANES * (j + 1)] = half_land[phase, j]
-
-        @pl.loop(0, 8)
-        def _(pair):
-            columns = pl.ds(pl.multiple_of(256 * pair, 256), 256)
-            product = jnp.dot(half_flat[...], east_all[:, columns], preferred_element_type=F32)
-            finish(2 * pair, product[:, :LANES])
-            finish(2 * pair + 1, product[:, LANES:])
+        for number, d_row in enumerate(ORDER):
+            row = from_row(back_copy, back_recv, phase, d_row)
+            left = jnp.concatenate([half_land[phase, 4 * row + c] for c in range(4)], axis=1)
+            depth = pl.ds(pl.multiple_of(512 * row, 512), 512)
+            if number < 3:
+                product = jnp.dot(left, east_all[depth, :], preferred_element_type=F32)
+                east_sum[...] = product if number == 0 else east_sum[...] + product
+                continue
+            for d_pair in range(8):
+                pair = lax.rem(lax.div(chip, 2) + d_pair, 8)
+                part = pl.ds(pl.multiple_of(256 * pair, 256), 256)
+                product = east_sum[:, part] + jnp.dot(left, east_all[depth, part], preferred_element_type=F32)
+                for h in (0, 1):
+                    finish(2 * pair + h, product[:, LANES * h:LANES * (h + 1)], d_pair == 0)
 
     loaded(mult, load_sem.at[0])
-
-    @pl.loop(0, CHUNKS)
-    def _(j):
+    for j in range(CHUNKS):
         strip_mine[4, j] = mult[j].astype(BF16)
-
-    there_start(0)
+    for offset in range(1, 16):
+        there_copy(0, plane(offset)[0]).start()
+    there_own(0)
     loaded(force, load_sem.at[2])
     pack(DIFF, force)
     swap_start(DIFF)
@@ -364,8 +453,9 @@
     swap_start(INCR)
     gather_first_ring()
     gather_own_second()
+    relay_across(DIFF)
+    relay_across(INCR)
     gather_far()
-    there_wait(0)
     swap_wait_number(DIFF, FROM_SAME)
 
     def put_own(j, value):
@@ -373,56 +463,64 @@
 
     each_wide(DIFF, 1, lambda j: force[j], put_own)
     load(forcing.at[0], force, load_sem.at[2])
+    relay_to_hub(DIFF)
+    relay_to_hub(INCR)
+    own_north.wait()
+    gather_rest()
+    north_product(0)
     swap_wait_number(DIFF, FROM_BEFORE)
+    relay_end(DIFF, 4)
 
     def put_prev(j, value):
         diff_prev[j + 1] = value
 
     each_wide(DIFF, 0, landed(DIFF, 0), put_prev)
     swap_wait_number(INCR, FROM_BEFORE)
+    relay_end(INCR, 4)
 
     def put_incr(j, value):
         incr_prev[j] = value
         work[j + 1] = value
 
     each_wide(INCR, 0, landed(INCR, 0), put_incr)
-    own_north.wait()
-    gather_rest()
-    north_product(0)
-    run_model(diff_prev)
-
-    def keep_model():
-        @pl.loop(0, CHUNKS)
-        def _(j):
-            moved = jnp.where(first, 0.0, work[j + 1, HALO:HALO + ROWS])
-            model[j] = force[j] - incr_own[j] + moved
-
+    run_steps(diff_prev, False)
     loaded(force, load_sem.at[2])
-    keep_model()
+    for j in range(CHUNKS):
+        model[j] = force[j] - incr_own[j] + jnp.where(first, 0.0, work[j + 1, HALO:HALO + ROWS])
     own_east.wait()
 
-    def update(j, product):
-        mult[j] = mult[j] + 0.5 * (model[j] - product)
-
-    east_product(0, update)
+    def update(phase):
+        def finish(j, product, own):
+            value = mult[j] + 0.5 * (model[j] - product)
+            mult[j] = value
+            rounded = value.astype(BF16)
+            strip_mine[low_of[phase + 1], j] = rounded
+            if not own:
+                there_copy(phase + 1, j).start()
+            else:
+                @pl.when(j != chip)
+                def _():
+                    there_copy(phase + 1, j).start()
+        return finish
+
+    east_product(0, update(0))
 
     for phase in range(1, PHASES):
         which = MULT - 1 + phase
         final = phase == PHASES - 1
+        there_own(phase)
         pack(which, mult)
-        there_start(phase)
         swap_start(which)
         swap_wait_number(which, FROM_SAME)
         each_wide(which, 1, lambda j: mult[j], put_work)
-        run_adjoint(diff_prev)
-        there_wait(phase)
-
-        @pl.loop(0, CHUNKS)
-        def _(j):
+        relay_across(which)
+        run_steps(diff_prev, True)
+        for j in range(CHUNKS):
             incr_prev[j] = incr_prev[j] - 0.5 * work[j + 1]
-
         north_product(phase)
+        relay_to_hub(which)
         swap_wait_number(which, FROM_BEFORE)
+        relay_end(which, 4)
 
         def put_before(j, value):
             value = jnp.where(inside, incr_prev[j] + 0.5 * value, 0.0)
@@ -430,54 +528,48 @@
             work[j + 1] = value
 
         each_wide(which, 0, landed(which, 0), put_before)
-        run_model(diff_prev)
-
-        @pl.loop(0, CHUNKS)
-        def _(j):
+        run_steps(diff_prev, False)
+        for j in range(CHUNKS):
             model[j] = force[j] + jnp.where(first, 0.0, work[j + 1, HALO:HALO + ROWS])
-
         swap_wait_number(which, FROM_AFTER)
+        relay_end(which, 3)
         each_wide(which, 2, landed(which, 1), put_work)
-        run_adjoint(diff_own)
-
-        @pl.loop(0, CHUNKS)
-        def _(j):
+        run_steps(diff_own, True)
+
+        def stored(source, target, j, sem):
+            columns = pl.ds(pl.multiple_of(LANES * j, LANES), LANES)
+            pltpu.make_async_copy(source, target.at[0, :, columns], sem).start()
+
+        for j in range(CHUNKS):
             grad = mult[j] - jnp.where(last, 0.0, work[j + 1, HALO:HALO + ROWS])
             incr = incr_own[j] + 0.5 * grad
             incr_own[j] = incr
             model[j] = model[j] - incr
             if final:
-                work[j + 1, HALO:HALO + ROWS] = grad
-
-        def stored(source, target, sem):
-            return [
-                pltpu.make_async_copy(source(j), target.at[0, :, pl.ds(LANES * j, LANES)], sem) for j in range(CHUNKS)
-            ]
+                force[j] = grad
+                stored(force.at[j], grad_out, j, out_sem.at[0])
 
         if not final:
-            east_product(phase, update)
+            east_product(phase, update(phase))
         else:
-            for copy in stored(lambda j: work.at[j + 1, pl.ds(HALO, ROWS)], grad_out, out_sem.at[0]):
-                copy.start()
-
-            def finish(j, product):
-                model[j] = model[j] - product
+            def finish(j, product, own):
+                mult[j] = model[j] - product
+                stored(mult.at[j], mult_out, j, out_sem.at[1])
 
             east_product(phase, finish)
-            for copy in stored(lambda j: model.at[j], mult_out, out_sem.at[1]):
-                copy.start()
 
     for copy in gather_sends:
         copy.wait_send()
     for phase in range(PHASES):
-        @pl.loop(1, 16)
-        def _(offset, phase=phase):
-            there_copy(phase, offset).wait_send()
-            back_copy(phase, offset).wait_send()
-        core_copy(phase).wait_send()
+        for offset in range(1, 16):
+            there_copy(phase, plane(offset)[0]).wait_send()
+            back_copy(phase, plane(offset)[0]).wait_send()
+        for row in range(4):
+            core_copy(phase, row).wait_send()
     for which in (DIFF, INCR, MULT, MULT + 1):
         for copy, sent, _ in swap_copies(which):
             pl.when(sent)(copy.wait_send)
+        relay_sent(which)
     pltpu.make_async_copy(model, model, out_sem.at[0]).wait()
     pltpu.make_async_copy(model, model, out_sem.at[1]).wait()
 
@@ -512,18 +604,24 @@
             pltpu.VMEM(strip, F32),
             pltpu.VMEM(strip, F32),
             pltpu.VMEM(strip, F32),
-            pltpu.VMEM((ROWS, 2048), BF16),
             pltpu.VMEM(strip, F32),
+            pltpu.VMEM((1024, LANES), F32),
+            pltpu.VMEM((ROWS, 2048), F32),
+            pltpu.VMEM((4, 4, ROWS, LANES), BF16),
+            pltpu.VMEM((4, 4, ROWS, LANES), BF16),
             dma((5,)),
             dma((pieces * 20,)),
             dma((pieces * 32,)),
             dma((PHASES, 16)),
             dma((PHASES, 16)),
-            dma((PHASES, 2)),
+            dma((PHASES, 4)),
+            dma((PHASES, 4)),
             dma((PHASES, 16)),
             dma((PHASES, 16)),
             dma((4, 8)),
             dma((4, 8)),
+            dma((4, 6)),
+            dma((4, 6)),
             dma((2,)),
         ],
         compiler_params=pltpu.CompilerParams(

time: 172 us -> 124 us (0.72)
  Pallas kernels: 164 us -> 116 us
    pallas_call x1, Pallas kernels: 164 us -> 116 us  [local(): pl.pallas_call(kernel, out_shape=(out, out), in_specs=[any_space] * 6, ou...]
where the time goes in v2:
time: 124 us
  Pallas kernels  116 us (94%)
  local copies, waits for them, and re-layouts  6.7 us (5%)
    pallas_call x1, Pallas kernels, local(): pl.pallas_call(kernel, out_shape=(out, out), in_specs=[any_space] * 6, ou...  116 us
    unnamed x12, local copies, waits for them, and re-layouts  6.7 us

profile of v2, /device:TPU:7, one launch (start us, length us, event | category | flops | bytes accessed | tf_op | source)
XLA Modules:
  0.0 123.5 jit_solution(8769955241992443366)
XLA Ops:
  0.6 0.0 copy-start
  0.6 1.0 copy-done
  1.7 0.0 copy-start.1
  1.7 1.0 copy-done.1
  2.7 0.0 copy-start.2
  2.7 1.0 copy-done.2
  3.8 0.0 copy-start.3
  3.8 1.0 copy-done.3
  4.8 0.0 copy-start.4
  4.8 0.9 copy-done.4
  5.8 116.2 %shard_map.77 = (f32[1,64,2048]{2,1,0:T(8,128)S(1)}, f32[1,64,2048]{2,1,0:T(8,128)S(1)}) custom-call(f32[1,64,2048]{2,1,0:T(8,128)S(1)} %copy-done, f32[1,64,2048]{2,1,0:T(8,128)S(1)} %copy-done.1, f32[1,64,2048]{2,1,0:T(8,128)S(1)} %copy-done.2, f32[1,64,2048]{2,1,0:T(8,128)S(1)} %copy-done.3, bf16[64,2048]{1,0:T(8,128)(2,1)S(1)} %copy-done.4, ...), custom_call_target="tpu_custom_call" | custom-call | tf_op jit(solution)/shard_map/pallas_call | solution.py:585
  121.9 0.8 copy.10
  122.7 0.8 copy.11
Async XLA Ops:
  0.6 1.0 copy-start
  1.7 1.0 copy-start.1
  2.7 1.0 copy-start.2
  3.8 1.0 copy-start.3
  4.8 0.9 copy-start.4

commit v3 on v2

--- a/solution.py
+++ b/solution.py
@@ -15,15 +15,15 @@
 
 ROWS, WIDE, CHUNKS, LANES = 64, 80, 16, 128
 HALO = 8
-GATHER_PARTS = ((0, 1024, "zy"), (1024, 1024, "yz"))
+GATHER_PARTS = ((0, 768, "zy"), (768, 512, "yz"), (1280, 768, "yzx"))
 
 DIFF, INCR, MULT = 0, 1, 2
 
 
 def kernel(forcing, mult_in, incr_in, diff_in, north, east, mult_out, grad_out,
            north_all, east_all, low_land, half_land, half_mine, strip_land, rim_land, strip_mine, rim_mine,
-           work, diff_prev, diff_own, incr_prev, incr_own, mult, force, model, north_sum, east_sum, relay_out, relay_in,
-           load_sem, gather_send, gather_recv, there_send, there_recv, core_send, core_recv, back_send, back_recv,
+           work, diff_prev, diff_own, incr_prev, incr_own, mult, force, model, grad_kept, north_sum, east_sum, relay_out, relay_in,
+           load_sem, gather_send, gather_recv, shared_send, shared_recv, there_send, there_recv, core_send, core_recv, back_send, back_recv,
            swap_send, swap_recv, relay_send, relay_recv, out_sem):
     sub, strip = lax.axis_index("sub"), lax.axis_index("strip")
     x, z_hi = lax.rem(sub, 4), lax.div(sub, 4)
@@ -55,20 +55,6 @@
     is_hub = sub == hub
     across = (lax.rem(sub + 4, 8), strip)
 
-    def load(source, target, sem):
-        for j in range(CHUNKS):
-            pltpu.make_async_copy(source.at[:, pl.ds(LANES * j, LANES)], target.at[j], sem).start()
-
-    def loaded(target, sem):
-        pltpu.make_async_copy(target, target, sem).wait()
-
-    load(mult_in.at[0], mult, load_sem.at[0])
-    load(incr_in.at[0], incr_own, load_sem.at[1])
-    load(diff_in.at[0], force, load_sem.at[2])
-    own_north = pltpu.make_async_copy(north, north_all.at[chip], load_sem.at[3])
-    own_north.start()
-    own_east = pltpu.make_async_copy(east, east_all, load_sem.at[4])
-    own_east.start()
     rim_land[...] = jnp.zeros_like(rim_land)
     for ref in (work, diff_prev, diff_own):
         ref[0] = jnp.zeros((WIDE, LANES), F32)
@@ -83,8 +69,10 @@
         greet(plane(offset)[1])
     greet(peer)
     greet(across)
+    for step in (-2, -1, 1, 2):
+        greet(along("z", step))
     for step in (-1, 1):
-        greet(along("z", step))
+        greet(device(lax.rem(x + step + 4, 4), y, z_all))
     near = [
         (-1, 0, ~first), (1, 0, ~last),
         (-1, -1, ~first & ~top), (-1, 1, ~first & ~bottom),
@@ -104,82 +92,133 @@
     def _():
         greet((hub, strip))
 
-    expected = 19 + jnp.where(is_hub, 3, 1)
+    expected = 23 + jnp.where(is_hub, 3, 1)
     for _, _, there in near:
         expected = expected + there.astype(jnp.int32)
+    def load(source, target, sem):
+        for j in range(CHUNKS):
+            pltpu.make_async_copy(source.at[:, pl.ds(LANES * j, LANES)], target.at[j], sem).start()
+
+    def loaded(target, sem):
+        pltpu.make_async_copy(target, target, sem).wait()
+
+    load(mult_in.at[0], mult, load_sem.at[0])
+    load(incr_in.at[0], incr_own, load_sem.at[1])
+    load(diff_in.at[0], force, load_sem.at[2])
+    shared = GATHER_PARTS[2][0]
+    own_rows = pl.ds(pl.multiple_of(16 * x, 16), 16)
+    own_north = [
+        pltpu.make_async_copy(north.at[:, pl.ds(0, shared)], north_all.at[chip, :, pl.ds(0, shared)], load_sem.at[3]),
+        pltpu.make_async_copy(
+            north.at[own_rows, pl.ds(shared, 2048 - shared)],
+            north_all.at[chip, own_rows, pl.ds(shared, 2048 - shared)], load_sem.at[5]),
+    ]
+    for copy in own_north:
+        copy.start()
+    own_east = pltpu.make_async_copy(east, east_all, load_sem.at[4])
+    own_east.start()
     pl.semaphore_wait(barrier, expected)
 
     gather_sends = []
 
-    def part_copy(part, piece, half, src, to, recv_at, sends):
-        start, size, _ = GATHER_PARTS[part]
+    def gather_copy(part, piece, half, source, to, recv_at, sends):
+        start, size, order = GATHER_PARTS[part]
         if half is not None:
-            start, size = start + half * (size // 2), size // 2
+            width = size // 2 // LANES * LANES
+            start, size = (start, width) if half == 0 else (start + width, size - width)
         columns = pl.ds(start, size)
-        source = (north if src else north_all.at[piece]).at[:, columns]
-        return remote(source, north_all.at[piece, :, columns], gather_send.at[sends], gather_recv.at[recv_at], to)
-
-    def slot(part, rel_a, rel_b, half=0):
-        return ((part * 4 + rel_a) * 4 + rel_b) * 2 + half
+        rows = pl.ds(pl.multiple_of(16 * x, 16), 16) if "x" in order else pl.ds(0, ROWS)
+        source = source.at[rows, columns] if source is north else source.at[piece, rows, columns]
+        return remote(source, north_all.at[piece, rows, columns], gather_send.at[sends], gather_recv.at[recv_at], to)
+
+    def slot(part, rel_a, rel_b, half):
+        return ((part * 4 + rel_a) * 4 + rel_b) * 2 + (half or 0)
 
     def piece_of(part, rel_a, rel_b):
-        rel_z, rel_y = (rel_a, rel_b) if GATHER_PARTS[part][2] == "zy" else (rel_b, rel_a)
+        rel_z, rel_y = (rel_a, rel_b) if GATHER_PARTS[part][2][0] == "z" else (rel_b, rel_a)
         return lax.rem(y + rel_y, 4) * 4 + lax.rem(z + rel_z, 4)
 
-    def gather_send_piece(part, rel_a, rel_b, dim_at, step, half=None):
-        dim = GATHER_PARTS[part][2][dim_at]
-        to_a, to_b = (rel_a, rel_b)
-        if dim_at == 0:
-            to_a = (rel_a - step) % 4
-        else:
-            to_b = (rel_b - step) % 4
-        copy = part_copy(
-            part, piece_of(part, rel_a, rel_b), half, (rel_a, rel_b) == (0, 0), along(dim, step),
-            slot(part, to_a, to_b, half or 0), len(gather_sends),
+    def gather_put(part, rel_a, rel_b, ring, step, half=None):
+        to_a, to_b = ((rel_a - step) % 4, rel_b) if ring == 0 else (rel_a, (rel_b - step) % 4)
+        copy = gather_copy(
+            part, piece_of(part, rel_a, rel_b), half, north if (rel_a, rel_b) == (0, 0) else north_all,
+            along(GATHER_PARTS[part][2][ring], step), slot(part, to_a, to_b, half), len(gather_sends),
         )
         copy.start()
         gather_sends.append(copy)
 
     def gather_wait(part, rel_a, rel_b, half=None):
-        part_copy(part, piece_of(part, rel_a, rel_b), half, False, peer, slot(part, rel_a, rel_b, half or 0), 0).wait_recv()
+        gather_copy(part, piece_of(part, rel_a, rel_b), half, north_all, peer, slot(part, rel_a, rel_b, half), 0).wait_recv()
 
     parts = range(len(GATHER_PARTS))
-    for part in parts:
-        for dim_at in (0, 1):
-            for step in (1, -1):
-                gather_send_piece(part, 0, 0, dim_at, step)
-
-    def gather_first_ring():
-        for rel, step in ((3, 1), (1, -1)):
-            for part in parts:
-                gather_wait(part, rel, 0)
-                gather_send_piece(part, rel, 0, 0, step, half=0 if step == 1 else 1)
-                gather_send_piece(part, rel, 0, 1, 1)
-                gather_send_piece(part, rel, 0, 1, -1)
-
-    def gather_own_second():
-        for rel, step in ((3, 1), (1, -1)):
-            for part in parts:
-                gather_wait(part, 0, rel)
-                gather_send_piece(part, 0, rel, 1, step, half=0 if step == 1 else 1)
-
-    def gather_far():
+
+    def gather_start():
         for part in parts:
-            gather_wait(part, 2, 0, 0)
-            gather_wait(part, 2, 0, 1)
-            gather_send_piece(part, 2, 0, 1, 1)
-            gather_send_piece(part, 2, 0, 1, -1)
-
-    def gather_rest():
-        for rel_a in (3, 1, 2):
+            gather_put(part, 0, 0, 0, 1)
+            gather_put(part, 0, 0, 0, -1)
+        for part in parts:
+            gather_put(part, 0, 0, 1, 1)
+            gather_put(part, 0, 0, 1, -1)
+            gather_put(part, 0, 0, 0, 2)
+
+    def gather_first(rel):
+        for part in parts:
+            gather_wait(part, rel, 0)
+            gather_put(part, rel, 0, 1, 1)
+            gather_put(part, rel, 0, 1, -1)
+
+    def gather_second(rel_a):
+        for part in parts:
             for rel, step in ((3, 1), (1, -1)):
-                for part in parts:
-                    gather_wait(part, rel_a, rel)
-                    gather_send_piece(part, rel_a, rel, 1, step, half=0 if step == 1 else 1)
-        for rel_a in (0, 3, 1, 2):
-            for part in parts:
-                gather_wait(part, rel_a, 2, 0)
-                gather_wait(part, rel_a, 2, 1)
+                gather_wait(part, rel_a, rel)
+                gather_put(part, rel_a, rel, 1, step, half=0 if step == 1 else 1)
+
+    def gather_far(rel_a):
+        for part in parts:
+            gather_wait(part, rel_a, 2, 0)
+            gather_wait(part, rel_a, 2, 1)
+
+    def shared_ref(rel_a, far, half):
+        start, size, _ = GATHER_PARTS[2]
+        if half is not None:
+            start, size = start + half * (size // 2), size // 2
+        at = lax.rem(y + rel_a, 4)
+        rows = pl.ds(pl.multiple_of(16 * lax.rem(x + far, 4), 16), 16)
+        return north_all.at[pl.ds(4 * at, 4), rows, pl.ds(start, size)]
+
+    def shared_put(rel_a, far, step, half=None):
+        ref = shared_ref(rel_a, far, half)
+        at = (rel_a * 4 + (far - step) % 4) * 2 + (half or 0)
+        copy = remote(ref, ref, shared_send.at[len(shared_sends)], shared_recv.at[at],
+                      device(lax.rem(x + step + 4, 4), y, z_all))
+        copy.start()
+        shared_sends.append(copy)
+
+    def shared_wait(rel_a, far, half=None):
+        ref = shared_ref(rel_a, far, half)
+        at = (rel_a * 4 + far) * 2 + (half or 0)
+        remote(ref, ref, shared_recv.at[at], shared_recv.at[at], peer).wait_recv()
+
+    shared_sends = []
+
+    def shared_start(rel_a):
+        for _ in parts[:1]:
+            shared_put(rel_a, 0, 1)
+            shared_put(rel_a, 0, -1)
+
+    def shared_on(rel_a):
+        for _ in parts[:1]:
+            shared_wait(rel_a, 3)
+            shared_put(rel_a, 3, 1, half=0)
+            shared_wait(rel_a, 1)
+            shared_put(rel_a, 1, -1, half=1)
+
+    def shared_end(rel_a):
+        for _ in parts[:1]:
+            shared_wait(rel_a, 2, 0)
+            shared_wait(rel_a, 2, 1)
+
+    gather_start()
 
     def swap_copies(which):
         copies = []
@@ -451,11 +490,16 @@
     loaded(incr_own, load_sem.at[1])
     pack(INCR, incr_own)
     swap_start(INCR)
-    gather_first_ring()
-    gather_own_second()
+    gather_first(3)
+    gather_first(1)
+    for copy in own_north:
+        copy.wait()
+    gather_second(0)
+    gather_first(2)
     relay_across(DIFF)
     relay_across(INCR)
-    gather_far()
+    gather_far(0)
+    shared_start(0)
     swap_wait_number(DIFF, FROM_SAME)
 
     def put_own(j, value):
@@ -465,8 +509,18 @@
     load(forcing.at[0], force, load_sem.at[2])
     relay_to_hub(DIFF)
     relay_to_hub(INCR)
-    own_north.wait()
-    gather_rest()
+    for rel_a in (3, 1):
+        gather_second(rel_a)
+        gather_far(rel_a)
+        shared_start(rel_a)
+    shared_on(0)
+    gather_second(2)
+    gather_far(2)
+    shared_start(2)
+    for rel_a in (3, 1, 2):
+        shared_on(rel_a)
+    for rel_a in (0, 3, 1, 2):
+        shared_end(rel_a)
     north_product(0)
     swap_wait_number(DIFF, FROM_BEFORE)
     relay_end(DIFF, 4)
@@ -519,6 +573,23 @@
             incr_prev[j] = incr_prev[j] - 0.5 * work[j + 1]
         north_product(phase)
         relay_to_hub(which)
+        def stored(source, target, j, sem):
+            columns = pl.ds(pl.multiple_of(LANES * j, LANES), LANES)
+            pltpu.make_async_copy(source, target.at[0, :, columns], sem).start()
+
+        def own_increments():
+            swap_wait_number(which, FROM_AFTER)
+            relay_end(which, 3)
+            each_wide(which, 2, landed(which, 1), put_work)
+            run_steps(diff_own, True)
+            for j in range(CHUNKS):
+                grad = mult[j] - jnp.where(last, 0.0, work[j + 1, HALO:HALO + ROWS])
+                incr_own[j] = incr_own[j] + 0.5 * grad
+                if final:
+                    grad_kept[j] = grad
+                    stored(grad_kept.at[j], grad_out, j, out_sem.at[0])
+
+        pl.when(sub != 3)(own_increments)
         swap_wait_number(which, FROM_BEFORE)
         relay_end(which, 4)
 
@@ -531,24 +602,9 @@
         run_steps(diff_prev, False)
         for j in range(CHUNKS):
             model[j] = force[j] + jnp.where(first, 0.0, work[j + 1, HALO:HALO + ROWS])
-        swap_wait_number(which, FROM_AFTER)
-        relay_end(which, 3)
-        each_wide(which, 2, landed(which, 1), put_work)
-        run_steps(diff_own, True)
-
-        def stored(source, target, j, sem):
-            columns = pl.ds(pl.multiple_of(LANES * j, LANES), LANES)
-            pltpu.make_async_copy(source, target.at[0, :, columns], sem).start()
-
+        pl.when(sub == 3)(own_increments)
         for j in range(CHUNKS):
-            grad = mult[j] - jnp.where(last, 0.0, work[j + 1, HALO:HALO + ROWS])
-            incr = incr_own[j] + 0.5 * grad
-            incr_own[j] = incr
-            model[j] = model[j] - incr
-            if final:
-                force[j] = grad
-                stored(force.at[j], grad_out, j, out_sem.at[0])
-
+            model[j] = model[j] - incr_own[j]
         if not final:
             east_product(phase, update(phase))
         else:
@@ -558,7 +614,7 @@
 
             east_product(phase, finish)
 
-    for copy in gather_sends:
+    for copy in gather_sends + shared_sends:
         copy.wait_send()
     for phase in range(PHASES):
         for offset in range(1, 16):
@@ -575,7 +631,7 @@
 
 
 def local(forcing, mult_start, incr_start, diffusivity, north_corr, east_corr):
-    any_space = pl.BlockSpec(memory_space=pl.ANY)
+    any_space = pl.BlockSpec(memory_space=pltpu.HBM)
     dma = pltpu.SemaphoreType.DMA
     strip = (CHUNKS, ROWS, LANES)
     wide = (CHUNKS, WIDE, LANES)
@@ -605,13 +661,16 @@
             pltpu.VMEM(strip, F32),
             pltpu.VMEM(strip, F32),
             pltpu.VMEM(strip, F32),
+            pltpu.VMEM(strip, F32),
             pltpu.VMEM((1024, LANES), F32),
             pltpu.VMEM((ROWS, 2048), F32),
             pltpu.VMEM((4, 4, ROWS, LANES), BF16),
             pltpu.VMEM((4, 4, ROWS, LANES), BF16),
-            dma((5,)),
-            dma((pieces * 20,)),
+            dma((6,)),
+            dma((pieces * 19,)),
             dma((pieces * 32,)),
+            dma((16,)),
+            dma((32,)),
             dma((PHASES, 16)),
             dma((PHASES, 16)),
             dma((PHASES, 4)),

time: 124 us -> 138 us (1.11)
  Pallas kernels: 116 us -> 130 us
    pallas_call x1, Pallas kernels: 116 us -> 130 us  [local(): pl.pallas_call(kernel, out_shape=(out, out), in_specs=[any_space] * 6, ou...]
where the time goes in v3:
time: 138 us; the launch traced here: 137 us
  Pallas kernels  130 us (94%)
  local copies, waits for them, and re-layouts  6.7 us (5%)
    pallas_call x1, Pallas kernels, local(): pl.pallas_call(kernel, out_shape=(out, out), in_specs=[any_space] * 6, ou...  130 us
    unnamed x12, local copies, waits for them, and re-layouts  6.7 us

profile of v3, /device:TPU:7, one launch (start us, length us, event | category | flops | bytes accessed | tf_op | source)
XLA Modules:
  0.0 137.3 jit_solution(10209835917343733105)
XLA Ops:
  0.6 0.0 copy-start
  0.6 1.0 copy-done
  1.7 0.0 copy-start.1
  1.7 1.0 copy-done.1
  2.7 0.0 copy-start.2
  2.7 1.0 copy-done.2
  3.8 0.0 copy-start.3
  3.8 1.0 copy-done.3
  4.8 0.0 copy-start.4
  4.8 0.9 copy-done.4
  5.8 129.9 %shard_map.77 = (f32[1,64,2048]{2,1,0:T(8,128)S(1)}, f32[1,64,2048]{2,1,0:T(8,128)S(1)}) custom-call(f32[1,64,2048]{2,1,0:T(8,128)S(1)} %copy-done, f32[1,64,2048]{2,1,0:T(8,128)S(1)} %copy-done.1, f32[1,64,2048]{2,1,0:T(8,128)S(1)} %copy-done.2, f32[1,64,2048]{2,1,0:T(8,128)S(1)} %copy-done.3, bf16[64,2048]{1,0:T(8,128)(2,1)S(1)} %copy-done.4, ...), custom_call_target="tpu_custom_call" | custom-call | tf_op jit(solution)/shard_map/pallas_call | solution.py:641
  135.7 0.8 copy.10
  136.5 0.8 copy.11
Async XLA Ops:
  0.6 1.0 copy-start
  1.7 1.0 copy-start.1
  2.7 1.0 copy-start.2
  3.8 1.0 copy-start.3
  4.8 0.9 copy-start.4

commit v4 on v3

--- a/solution.py
+++ b/solution.py
@@ -173,8 +173,8 @@
                 gather_wait(part, rel_a, rel)
                 gather_put(part, rel_a, rel, 1, step, half=0 if step == 1 else 1)
 
-    def gather_far(rel_a):
-        for part in parts:
+    def gather_far(rel_a, some):
+        for part in some:
             gather_wait(part, rel_a, 2, 0)
             gather_wait(part, rel_a, 2, 1)
 
@@ -427,7 +427,7 @@
 
     ORDER = (0, 1, 3, 2)
 
-    def north_product(phase):
+    def north_product(phase, when_heard=lambda: None):
         rows = []
 
         def arrive(d_row):
@@ -442,6 +442,8 @@
         for number in range(4):
             if number < 3:
                 arrive(ORDER[number + 1])
+            if number == 2:
+                when_heard()
             row = rows[number]
             core_copy(phase, row).wait_recv()
             depth = pl.ds(pl.multiple_of(512 * row, 512), 512)
@@ -486,20 +488,29 @@
     there_own(0)
     loaded(force, load_sem.at[2])
     pack(DIFF, force)
-    swap_start(DIFF)
     loaded(incr_own, load_sem.at[1])
     pack(INCR, incr_own)
-    swap_start(INCR)
     gather_first(3)
     gather_first(1)
     for copy in own_north:
         copy.wait()
     gather_second(0)
     gather_first(2)
+    swap_start(DIFF)
+    swap_start(INCR)
+    gather_second(3)
+    gather_second(1)
+    gather_far(0, parts[2:])
+    shared_start(0)
+    gather_second(2)
     relay_across(DIFF)
     relay_across(INCR)
-    gather_far(0)
-    shared_start(0)
+    for rel_a in (3, 1):
+        gather_far(rel_a, parts[2:])
+        shared_start(rel_a)
+    shared_on(0)
+    gather_far(2, parts[2:])
+    shared_start(2)
     swap_wait_number(DIFF, FROM_SAME)
 
     def put_own(j, value):
@@ -507,19 +518,13 @@
 
     each_wide(DIFF, 1, lambda j: force[j], put_own)
     load(forcing.at[0], force, load_sem.at[2])
+    shared_on(3)
+    shared_on(1)
     relay_to_hub(DIFF)
     relay_to_hub(INCR)
-    for rel_a in (3, 1):
-        gather_second(rel_a)
-        gather_far(rel_a)
-        shared_start(rel_a)
-    shared_on(0)
-    gather_second(2)
-    gather_far(2)
-    shared_start(2)
-    for rel_a in (3, 1, 2):
-        shared_on(rel_a)
+    shared_on(2)
     for rel_a in (0, 3, 1, 2):
+        gather_far(rel_a, parts[:2])
         shared_end(rel_a)
     north_product(0)
     swap_wait_number(DIFF, FROM_BEFORE)
@@ -567,12 +572,10 @@
         swap_start(which)
         swap_wait_number(which, FROM_SAME)
         each_wide(which, 1, lambda j: mult[j], put_work)
-        relay_across(which)
         run_steps(diff_prev, True)
         for j in range(CHUNKS):
             incr_prev[j] = incr_prev[j] - 0.5 * work[j + 1]
-        north_product(phase)
-        relay_to_hub(which)
+        north_product(phase, lambda: relay_across(which))
         def stored(source, target, j, sem):
             columns = pl.ds(pl.multiple_of(LANES * j, LANES), LANES)
             pltpu.make_async_copy(source, target.at[0, :, columns], sem).start()
@@ -590,6 +593,7 @@
                     stored(grad_kept.at[j], grad_out, j, out_sem.at[0])
 
         pl.when(sub != 3)(own_increments)
+        relay_to_hub(which)
         swap_wait_number(which, FROM_BEFORE)
         relay_end(which, 4)
 
@@ -684,7 +688,7 @@
             dma((2,)),
         ],
         compiler_params=pltpu.CompilerParams(
-            collective_id=0, has_side_effects=True, vmem_limit_bytes=48 * 2**20
+            collective_id=0, has_side_effects=True, vmem_limit_bytes=60 * 2**20
         ),
     )(forcing, mult_start, incr_start, diffusivity, north_corr, east_corr)
 

time: 138 us -> 128 us (0.928)
  Pallas kernels: 130 us -> 122 us
  local copies, waits for them, and re-layouts: 6.7 us -> 3.74 us
    pallas_call x1, Pallas kernels: 130 us -> 122 us  [local(): pl.pallas_call(kernel, out_shape=(out, out), in_specs=[any_space] * 6, ou...]
    unnamed x12 -> x2, local copies, waits for them, and re-layouts: 6.7 us -> 3.74 us
where the time goes in v4:
time: 128 us; the launch traced here: 126 us
  Pallas kernels  122 us (95%)
  local copies, waits for them, and re-layouts  3.74 us (3%)
    pallas_call x1, Pallas kernels, local(): pl.pallas_call(kernel, out_shape=(out, out), in_specs=[any_space] * 6, ou...  122 us
    unnamed x2, local copies, waits for them, and re-layouts  3.74 us

profile of v4, /device:TPU:7, one launch (start us, length us, event | category | flops | bytes accessed | tf_op | source)
XLA Modules:
  0.0 126.3 jit_solution(13371618573487584394)
XLA Ops:
  0.6 121.9 %shard_map.77 = (f32[1,64,2048]{2,1,0:T(8,128)}, f32[1,64,2048]{2,1,0:T(8,128)}) custom-call(f32[1,64,2048]{2,1,0:T(8,128)} %forcing.1, f32[1,64,2048]{2,1,0:T(8,128)} %mult_in.1, f32[1,64,2048]{2,1,0:T(8,128)} %incr_in.1, f32[1,64,2048]{2,1,0:T(8,128)} %diff_in.1, bf16[64,2048]{1,0:T(8,128)(2,1)} %north.1, bf16[2048,2048]{1,0:T(8,128)(2,1)} %east.1), custom_call_target="tpu_custom_call" | custom-call | tf_op jit(solution)/shard_map/pallas_call | solution.py:645
  122.5 1.9 %copy.10 = f32[1,64,2048]{2,1,0:T(8,128)} copy(f32[1,64,2048]{2,1,0:T(8,128)} %get-tuple-element.4) | data formatting | bytes 1048576
  124.4 1.9 %copy.11 = f32[1,64,2048]{2,1,0:T(8,128)} copy(f32[1,64,2048]{2,1,0:T(8,128)} %get-tuple-element.5) | data formatting | bytes 1048576

commit v5 on v2

--- a/solution.py
+++ b/solution.py
@@ -55,24 +55,7 @@
     is_hub = sub == hub
     across = (lax.rem(sub + 4, 8), strip)
 
-    def load(source, target, sem):
-        for j in range(CHUNKS):
-            pltpu.make_async_copy(source.at[:, pl.ds(LANES * j, LANES)], target.at[j], sem).start()
-
-    def loaded(target, sem):
-        pltpu.make_async_copy(target, target, sem).wait()
-
-    load(mult_in.at[0], mult, load_sem.at[0])
-    load(incr_in.at[0], incr_own, load_sem.at[1])
-    load(diff_in.at[0], force, load_sem.at[2])
-    own_north = pltpu.make_async_copy(north, north_all.at[chip], load_sem.at[3])
-    own_north.start()
-    own_east = pltpu.make_async_copy(east, east_all, load_sem.at[4])
-    own_east.start()
     rim_land[...] = jnp.zeros_like(rim_land)
-    for ref in (work, diff_prev, diff_own):
-        ref[0] = jnp.zeros((WIDE, LANES), F32)
-        ref[CHUNKS + 1] = jnp.zeros((WIDE, LANES), F32)
 
     barrier = pltpu.get_barrier_semaphore()
 
@@ -107,17 +90,31 @@
     expected = 19 + jnp.where(is_hub, 3, 1)
     for _, _, there in near:
         expected = expected + there.astype(jnp.int32)
+    def load(source, target, sem):
+        for j in range(CHUNKS):
+            pltpu.make_async_copy(source.at[:, pl.ds(LANES * j, LANES)], target.at[j], sem).start()
+
+    def loaded(target, sem):
+        pltpu.make_async_copy(target, target, sem).wait()
+
+    own_north = pltpu.make_async_copy(north, north_all.at[chip], load_sem.at[3])
+    own_north.start()
+    load(mult_in.at[0], mult, load_sem.at[0])
+    load(incr_in.at[0], incr_own, load_sem.at[1])
+    load(diff_in.at[0], force, load_sem.at[2])
+    own_east = pltpu.make_async_copy(east, east_all, load_sem.at[4])
+    own_east.start()
+
     pl.semaphore_wait(barrier, expected)
 
     gather_sends = []
 
-    def part_copy(part, piece, half, src, to, recv_at, sends):
+    def part_copy(part, piece, half, to, recv_at, sends):
         start, size, _ = GATHER_PARTS[part]
         if half is not None:
             start, size = start + half * (size // 2), size // 2
         columns = pl.ds(start, size)
-        source = (north if src else north_all.at[piece]).at[:, columns]
-        return remote(source, north_all.at[piece, :, columns], gather_send.at[sends], gather_recv.at[recv_at], to)
+        return remote(north_all.at[piece, :, columns], north_all.at[piece, :, columns], gather_send.at[sends], gather_recv.at[recv_at], to)
 
     def slot(part, rel_a, rel_b, half=0):
         return ((part * 4 + rel_a) * 4 + rel_b) * 2 + half
@@ -134,16 +131,17 @@
         else:
             to_b = (rel_b - step) % 4
         copy = part_copy(
-            part, piece_of(part, rel_a, rel_b), half, (rel_a, rel_b) == (0, 0), along(dim, step),
+            part, piece_of(part, rel_a, rel_b), half, along(dim, step),
             slot(part, to_a, to_b, half or 0), len(gather_sends),
         )
         copy.start()
         gather_sends.append(copy)
 
     def gather_wait(part, rel_a, rel_b, half=None):
-        part_copy(part, piece_of(part, rel_a, rel_b), half, False, peer, slot(part, rel_a, rel_b, half or 0), 0).wait_recv()
+        part_copy(part, piece_of(part, rel_a, rel_b), half, peer, slot(part, rel_a, rel_b, half or 0), 0).wait_recv()
 
     parts = range(len(GATHER_PARTS))
+    own_north.wait()
     for part in parts:
         for dim_at in (0, 1):
             for step in (1, -1):
@@ -170,16 +168,18 @@
             gather_send_piece(part, 2, 0, 1, 1)
             gather_send_piece(part, 2, 0, 1, -1)
 
-    def gather_rest():
-        for rel_a in (3, 1, 2):
+    def gather_rest(which):
+        for rel_a in which:
             for rel, step in ((3, 1), (1, -1)):
                 for part in parts:
                     gather_wait(part, rel_a, rel)
                     gather_send_piece(part, rel_a, rel, 1, step, half=0 if step == 1 else 1)
-        for rel_a in (0, 3, 1, 2):
-            for part in parts:
-                gather_wait(part, rel_a, 2, 0)
-                gather_wait(part, rel_a, 2, 1)
+
+    def gather_row(d_row):
+        pieces = [(1, d_row, 2)] + ([(0, rel_a, 2) for rel_a in range(4)] if d_row == 2 else [])
+        for part, rel_a, rel_b in pieces:
+            gather_wait(part, rel_a, rel_b, 0)
+            gather_wait(part, rel_a, rel_b, 1)
 
     def swap_copies(which):
         copies = []
@@ -388,6 +388,17 @@
 
     ORDER = (0, 1, 3, 2)
 
+    def half_back(phase, to_row, d_row, product):
+        half_mine[phase, pl.ds(4 * to_row, 4)] = product.astype(BF16).reshape(4, ROWS, LANES)
+        for d_z in range(1 if d_row == 0 else 0, 4):
+            back_copy(phase, to_row * 4 + lax.rem(z + d_z, 4)).start()
+
+    def arrive_all(phase):
+        rows = [from_row(there_copy, there_recv, phase, d_row) for d_row in ORDER]
+        for row in rows:
+            core_copy(phase, row).start()
+        return rows
+
     def north_product(phase):
         rows = []
 
@@ -417,10 +428,7 @@
                 product = jnp.dot(
                     north_all[pl.ds(4 * to_row, 4), :, depth].reshape(256, 512), columns(row),
                     preferred_element_type=F32)
-                half = (north_sum[part, :] + product).astype(BF16).reshape(4, ROWS, LANES)
-                half_mine[phase, pl.ds(4 * to_row, 4)] = half
-                for d_z in range(1 if d_row == 0 else 0, 4):
-                    back_copy(phase, to_row * 4 + lax.rem(z + d_z, 4)).start()
+                half_back(phase, to_row, d_row, north_sum[part, :] + product)
         half_land[phase, chip] = half_mine[phase, chip]
 
     def east_product(phase, finish):
@@ -465,9 +473,18 @@
     load(forcing.at[0], force, load_sem.at[2])
     relay_to_hub(DIFF)
     relay_to_hub(INCR)
-    own_north.wait()
-    gather_rest()
-    north_product(0)
+    gather_rest((3, 1))
+    low_rows = arrive_all(0)
+    gather_rest((2,))
+    for row in low_rows:
+        core_copy(0, row).wait_recv()
+    for d_row in (0, 1, 3, 2):
+        gather_row(d_row)
+        to_row = lax.rem(y + d_row, 4)
+        half_back(0, to_row, d_row, jnp.dot(
+            north_all[pl.ds(4 * to_row, 4)].reshape(256, 2048), low_land[0].reshape(2048, LANES),
+            preferred_element_type=F32))
+    half_land[0, chip] = half_mine[0, chip]
     swap_wait_number(DIFF, FROM_BEFORE)
     relay_end(DIFF, 4)
 
@@ -575,7 +592,7 @@
 
 
 def local(forcing, mult_start, incr_start, diffusivity, north_corr, east_corr):
-    any_space = pl.BlockSpec(memory_space=pl.ANY)
+    any_space = pl.BlockSpec(memory_space=pltpu.HBM)
     dma = pltpu.SemaphoreType.DMA
     strip = (CHUNKS, ROWS, LANES)
     wide = (CHUNKS, WIDE, LANES)
@@ -625,7 +642,7 @@
             dma((2,)),
         ],
         compiler_params=pltpu.CompilerParams(
-            collective_id=0, has_side_effects=True, vmem_limit_bytes=48 * 2**20
+            collective_id=0, has_side_effects=True, vmem_limit_bytes=60 * 2**20
         ),
     )(forcing, mult_start, incr_start, diffusivity, north_corr, east_corr)
 

time: 124 us -> 116 us (0.935)
  Pallas kernels: 116 us -> 111 us
  local copies, waits for them, and re-layouts: 6.7 us -> 3.74 us
    pallas_call x1, Pallas kernels: 116 us -> 111 us  [local(): pl.pallas_call(kernel, out_shape=(out, out), in_specs=[any_space] * 6, ou...]
    unnamed x12 -> x2, local copies, waits for them, and re-layouts: 6.7 us -> 3.74 us
where the time goes in v5:
time: 116 us
  Pallas kernels  111 us (96%)
  local copies, waits for them, and re-layouts  3.74 us (3%)
    pallas_call x1, Pallas kernels, local(): pl.pallas_call(kernel, out_shape=(out, out), in_specs=[any_space] * 6, ou...  111 us
    unnamed x2, local copies, waits for them, and re-layouts  3.74 us

profile of v5, /device:TPU:7, one launch (start us, length us, event | category | flops | bytes accessed | tf_op | source)
XLA Modules:
  0.0 115.6 jit_solution(13471993805770199866)
XLA Ops:
  0.6 111.2 %shard_map.77 = (f32[1,64,2048]{2,1,0:T(8,128)}, f32[1,64,2048]{2,1,0:T(8,128)}) custom-call(f32[1,64,2048]{2,1,0:T(8,128)} %forcing.1, f32[1,64,2048]{2,1,0:T(8,128)} %mult_in.1, f32[1,64,2048]{2,1,0:T(8,128)} %incr_in.1, f32[1,64,2048]{2,1,0:T(8,128)} %diff_in.1, bf16[64,2048]{1,0:T(8,128)(2,1)} %north.1, bf16[2048,2048]{1,0:T(8,128)(2,1)} %east.1), custom_call_target="tpu_custom_call" | custom-call | tf_op jit(solution)/shard_map/pallas_call | solution.py:602
  111.8 1.9 %copy.10 = f32[1,64,2048]{2,1,0:T(8,128)} copy(f32[1,64,2048]{2,1,0:T(8,128)} %get-tuple-element.4) | data formatting | bytes 1048576
  113.7 1.9 %copy.11 = f32[1,64,2048]{2,1,0:T(8,128)} copy(f32[1,64,2048]{2,1,0:T(8,128)} %get-tuple-element.5) | data formatting | bytes 1048576

commit v6 on v5

--- a/solution.py
+++ b/solution.py
@@ -15,7 +15,7 @@
 
 ROWS, WIDE, CHUNKS, LANES = 64, 80, 16, 128
 HALO = 8
-GATHER_PARTS = ((0, 1024, "zy"), (1024, 1024, "yz"))
+GATHER_PARTS = ((0, 1280, "zy"), (1280, 768, "yz"))
 
 DIFF, INCR, MULT = 0, 1, 2
 
@@ -455,15 +455,17 @@
     there_own(0)
     loaded(force, load_sem.at[2])
     pack(DIFF, force)
-    swap_start(DIFF)
     loaded(incr_own, load_sem.at[1])
     pack(INCR, incr_own)
-    swap_start(INCR)
     gather_first_ring()
     gather_own_second()
+    gather_far()
+    swap_start(DIFF)
+    swap_start(INCR)
+    gather_rest((3, 1))
+    low_rows = arrive_all(0)
     relay_across(DIFF)
     relay_across(INCR)
-    gather_far()
     swap_wait_number(DIFF, FROM_SAME)
 
     def put_own(j, value):
@@ -471,11 +473,9 @@
 
     each_wide(DIFF, 1, lambda j: force[j], put_own)
     load(forcing.at[0], force, load_sem.at[2])
+    gather_rest((2,))
     relay_to_hub(DIFF)
     relay_to_hub(INCR)
-    gather_rest((3, 1))
-    low_rows = arrive_all(0)
-    gather_rest((2,))
     for row in low_rows:
         core_copy(0, row).wait_recv()
     for d_row in (0, 1, 3, 2):

time: 116 us -> 112 us (0.966); the launches traced: 116 us -> 110 us
  Pallas kernels: 111 us -> 106 us
    pallas_call x1, Pallas kernels: 111 us -> 106 us  [local(): pl.pallas_call(kernel, out_shape=(out, out), in_specs=[any_space] * 6, ou...]
where the time goes in v6:
time: 112 us; the launch traced here: 110 us
  Pallas kernels  106 us (95%)
  local copies, waits for them, and re-layouts  3.74 us (3%)
    pallas_call x1, Pallas kernels, local(): pl.pallas_call(kernel, out_shape=(out, out), in_specs=[any_space] * 6, ou...  106 us
    unnamed x2, local copies, waits for them, and re-layouts  3.74 us

profile of v6, /device:TPU:7, one launch (start us, length us, event | category | flops | bytes accessed | tf_op | source)
XLA Modules:
  0.0 110.0 jit_solution(143826166049318601)
XLA Ops:
  0.6 105.7 %shard_map.77 = (f32[1,64,2048]{2,1,0:T(8,128)}, f32[1,64,2048]{2,1,0:T(8,128)}) custom-call(f32[1,64,2048]{2,1,0:T(8,128)} %forcing.1, f32[1,64,2048]{2,1,0:T(8,128)} %mult_in.1, f32[1,64,2048]{2,1,0:T(8,128)} %incr_in.1, f32[1,64,2048]{2,1,0:T(8,128)} %diff_in.1, bf16[64,2048]{1,0:T(8,128)(2,1)} %north.1, bf16[2048,2048]{1,0:T(8,128)(2,1)} %east.1), custom_call_target="tpu_custom_call" | custom-call | tf_op jit(solution)/shard_map/pallas_call | solution.py:602
  106.3 1.9 %copy.10 = f32[1,64,2048]{2,1,0:T(8,128)} copy(f32[1,64,2048]{2,1,0:T(8,128)} %get-tuple-element.4) | data formatting | bytes 1048576
  108.2 1.9 %copy.11 = f32[1,64,2048]{2,1,0:T(8,128)} copy(f32[1,64,2048]{2,1,0:T(8,128)} %get-tuple-element.5) | data formatting | bytes 1048576

commit v7 on v6

--- a/solution.py
+++ b/solution.py
@@ -22,7 +22,7 @@
 
 def kernel(forcing, mult_in, incr_in, diff_in, north, east, mult_out, grad_out,
            north_all, east_all, low_land, half_land, half_mine, strip_land, rim_land, strip_mine, rim_mine,
-           work, diff_prev, diff_own, incr_prev, incr_own, mult, force, model, north_sum, east_sum, relay_out, relay_in,
+           work, diff_prev, diff_own, incr_prev, incr_own, mult, force, model, grad_kept, north_sum, east_sum, relay_out, relay_in,
            load_sem, gather_send, gather_recv, there_send, there_recv, core_send, core_recv, back_send, back_recv,
            swap_send, swap_recv, relay_send, relay_recv, out_sem):
     sub, strip = lax.axis_index("sub"), lax.axis_index("strip")
@@ -206,9 +206,14 @@
         return copies
 
     def swap_start(which):
+        copies = swap_copies(which)
+        soon = {DIFF: (3, 4), INCR: ()}.get(which, (4, 5))
+        for at in soon:
+            pl.when(copies[at][1])(copies[at][0].start)
         relay_from_hub(which)
-        for copy, sent, _ in swap_copies(which):
-            pl.when(sent)(copy.start)
+        for at, (copy, sent, _) in enumerate(copies):
+            if at not in soon:
+                pl.when(sent)(copy.start)
 
     def swap_wait_number(which, numbers):
         copies = swap_copies(which)
@@ -536,6 +541,23 @@
             incr_prev[j] = incr_prev[j] - 0.5 * work[j + 1]
         north_product(phase)
         relay_to_hub(which)
+        def stored(source, target, j, sem):
+            columns = pl.ds(pl.multiple_of(LANES * j, LANES), LANES)
+            pltpu.make_async_copy(source, target.at[0, :, columns], sem).start()
+
+        def own_increments():
+            swap_wait_number(which, FROM_AFTER)
+            relay_end(which, 3)
+            each_wide(which, 2, landed(which, 1), put_work)
+            run_steps(diff_own, True)
+            for j in range(CHUNKS):
+                grad = mult[j] - jnp.where(last, 0.0, work[j + 1, HALO:HALO + ROWS])
+                incr_own[j] = incr_own[j] + 0.5 * grad
+                if final:
+                    grad_kept[j] = grad
+                    stored(grad_kept.at[j], grad_out, j, out_sem.at[0])
+
+        pl.when(sub != 3)(own_increments)
         swap_wait_number(which, FROM_BEFORE)
         relay_end(which, 4)
 
@@ -548,24 +570,9 @@
         run_steps(diff_prev, False)
         for j in range(CHUNKS):
             model[j] = force[j] + jnp.where(first, 0.0, work[j + 1, HALO:HALO + ROWS])
-        swap_wait_number(which, FROM_AFTER)
-        relay_end(which, 3)
-        each_wide(which, 2, landed(which, 1), put_work)
-        run_steps(diff_own, True)
-
-        def stored(source, target, j, sem):
-            columns = pl.ds(pl.multiple_of(LANES * j, LANES), LANES)
-            pltpu.make_async_copy(source, target.at[0, :, columns], sem).start()
-
+        pl.when(sub == 3)(own_increments)
         for j in range(CHUNKS):
-            grad = mult[j] - jnp.where(last, 0.0, work[j + 1, HALO:HALO + ROWS])
-            incr = incr_own[j] + 0.5 * grad
-            incr_own[j] = incr
-            model[j] = model[j] - incr
-            if final:
-                force[j] = grad
-                stored(force.at[j], grad_out, j, out_sem.at[0])
-
+            model[j] = model[j] - incr_own[j]
         if not final:
             east_product(phase, update(phase))
         else:
@@ -622,6 +629,7 @@
             pltpu.VMEM(strip, F32),
             pltpu.VMEM(strip, F32),
             pltpu.VMEM(strip, F32),
+            pltpu.VMEM(strip, F32),
             pltpu.VMEM((1024, LANES), F32),
             pltpu.VMEM((ROWS, 2048), F32),
             pltpu.VMEM((4, 4, ROWS, LANES), BF16),

time: 112 us -> 111 us (level)
  Pallas kernels: 106 us -> 104 us
    pallas_call x1, Pallas kernels: 106 us -> 104 us  [local(): pl.pallas_call(kernel, out_shape=(out, out), in_specs=[any_space] * 6, ou...]
where the time goes in v7:
time: 111 us; the launch traced here: 109 us
  Pallas kernels  104 us (94%)
  local copies, waits for them, and re-layouts  3.74 us (3%)
    pallas_call x1, Pallas kernels, local(): pl.pallas_call(kernel, out_shape=(out, out), in_specs=[any_space] * 6, ou...  104 us
    unnamed x2, local copies, waits for them, and re-layouts  3.74 us

profile of v7, /device:TPU:7, one launch (start us, length us, event | category | flops | bytes accessed | tf_op | source)
XLA Modules:
  0.0 108.5 jit_solution(14187959590513734975)
XLA Ops:
  0.6 104.2 %shard_map.77 = (f32[1,64,2048]{2,1,0:T(8,128)}, f32[1,64,2048]{2,1,0:T(8,128)}) custom-call(f32[1,64,2048]{2,1,0:T(8,128)} %forcing.1, f32[1,64,2048]{2,1,0:T(8,128)} %mult_in.1, f32[1,64,2048]{2,1,0:T(8,128)} %incr_in.1, f32[1,64,2048]{2,1,0:T(8,128)} %diff_in.1, bf16[64,2048]{1,0:T(8,128)(2,1)} %north.1, bf16[2048,2048]{1,0:T(8,128)(2,1)} %east.1), custom_call_target="tpu_custom_call" | custom-call | tf_op jit(solution)/shard_map/pallas_call | solution.py:609
  104.8 1.9 %copy.10 = f32[1,64,2048]{2,1,0:T(8,128)} copy(f32[1,64,2048]{2,1,0:T(8,128)} %get-tuple-element.4) | data formatting | bytes 1048576
  106.7 1.9 %copy.11 = f32[1,64,2048]{2,1,0:T(8,128)} copy(f32[1,64,2048]{2,1,0:T(8,128)} %get-tuple-element.5) | data formatting | bytes 1048576
